TPU v7x, 32 devices: a whole 2x2x4 slice. The times are simulated.
32 devices in a mesh: frame: 4 (over y, x), head: 4 (over z), dp: 2 (over core).
Axes of the slice: x: 2, y: 2, z: 4, core: 2. Of those that a mesh axis runs over, the one named last changes fastest.
Arguments:
- latent: bfloat16 [16, 8, 24, 5120], P(('dp', 'frame'), 'head'), parts along dimension 0, may hold values from -6 to 6, as said below
- pose_maps: bfloat16 [16, 16, 48, 256], P(('dp', 'frame'), 'head'), parts along dimension 0, may hold values from -6 to 6
- conv_weight: bfloat16 [3, 3, 3, 256, 320], replicated, may hold values from -0.078125 to 0.078125
- conv_bias: float32 [320], replicated, may hold values from -3 to 3
- pose_proj: bfloat16 [320, 5120], replicated, may hold values from -0.3125 to 0.3125
- w_qkv: bfloat16 [5120, 20, 3, 128], P('frame', 'head'), may hold values from -2 to 2
- w_out: bfloat16 [20, 128, 5120], P('head'), may hold values from -1 to 1
- clip_lengths: int32 [6], P('dp'), parts along dimension 0, may hold values from 1 to 4, 8 in all
- block_ids: int32 [16], P('dp'), parts along dimension 0, may hold values from 0 to 3, never falling along the last dimension, each value on 1 to 3 neighbouring positions
Outputs:
- attended: bfloat16 [16, 8, 24, 5120], P(('dp', 'frame'), 'head'), parts along dimension 0
There are 2 independent parts, one for each index of `dp`. A program takes and returns all parts, laid end to end along the dimension named above; an argument that names none is the same for every part. Nothing has to cross between parts.
Inputs may be any that keep to these rules, and one draw needn't show every extreme that they name: `clip_lengths`: the clips together cover all 8 frames; the longest clip has exactly 4 frames. `block_ids`: never falls along the frames; every block id in the range is used, by at most 3 consecutive frames. `latent`: activations of order one.
All inputs are finite; a program needn't handle non-finite values.
Results may differ from a plain program's by a relative error of at most 0.017.
Values may be sent and summed in bfloat16 or wider, within the bound.
No kernel may reach another device: no remote copies, remote signals or barrier semaphores. Data moves between devices by JAX's collectives and lax.ppermute only.
A program may use at most 128 MiB of HBM per device.

v0:
```python
import jax
import jax.numpy as jnp
from jax import lax
from jax.experimental import pallas as pl
from jax.experimental.pallas import tpu as pltpu
from jax.sharding import PartitionSpec as P

NEG_FILL = -1e30
MIB = 1 << 20
F32 = jnp.float32
BF16 = jnp.bfloat16
PLANE = 4
FIRST_COLUMNS = 8


def cost(flops, moved, exps=0):
    return pl.CostEstimate(flops=int(flops), bytes_accessed=int(moved), transcendentals=int(exps))


def shifted(value, axis, steps):
    count = lax.axis_size(axis)
    leading, last = (max(0, -steps), min(count, count - steps))
    return lax.ppermute(value, axis, [(source, source + steps) for source in range(leading, last)])


def frame_tables(clip_lengths, frame_count):
    clip_ends = jnp.cumsum(clip_lengths)
    clip_starts = clip_ends - clip_lengths
    frame_index = jnp.arange(frame_count, dtype=jnp.int32)
    clip_of = jnp.sum((frame_index[:, None] >= clip_ends[None, :]).astype(jnp.int32), axis=1)
    clip_match = clip_of[:, None] == jnp.arange(clip_lengths.shape[0], dtype=jnp.int32)[None, :]
    start_of = jnp.sum(jnp.where(clip_match, clip_starts[None, :], 0), axis=1)
    return (clip_of, start_of)


def guide_features(latent, pose_maps, conv_weight, conv_bias, pose_proj, start_of, first_frame):
    frames_dev = pose_maps.shape[0]
    upper_row = shifted(pose_maps[:, -1:], "head", 1)
    rows_ext = jnp.concatenate([upper_row, pose_maps], axis=1)
    left_column = jnp.zeros(rows_ext.shape[:2] + (1, rows_ext.shape[3]), rows_ext.dtype)
    cols_ext = jnp.concatenate([left_column, rows_ext], axis=2)
    earlier = shifted(cols_ext, "frame", 1)
    extended = jnp.concatenate([earlier, cols_ext], axis=0)
    out_rows = pose_maps.shape[1] // 2
    out_cols = pose_maps.shape[2] // 2
    frame_ids = first_frame + jnp.arange(frames_dev, dtype=jnp.int32)
    starts_here = lax.dynamic_slice_in_dim(start_of, first_frame, frames_dev)
    tap_list = []
    for step_a in range(3):
        keep_mask = (frame_ids - 2 + step_a >= starts_here).astype(pose_maps.dtype)[
            :, None, None, None
        ]
        frames_tap = extended[step_a : step_a + frames_dev] * keep_mask
        for step_b in range(3):
            for step_e in range(3):
                tap_list.append(
                    frames_tap[
                        :,
                        step_b : step_b + 2 * out_rows - 1 : 2,
                        step_e : step_e + 2 * out_cols - 1 : 2,
                    ]
                )
    stacked = jnp.concatenate(tap_list, axis=3)
    kernel = conv_weight.reshape(-1, conv_weight.shape[-1])
    summed = jnp.dot(stacked, kernel, preferred_element_type=jnp.float32) + conv_bias
    feature = jax.nn.silu(summed).astype(jnp.bfloat16)
    guided = latent.astype(jnp.float32) + jnp.dot(
        feature, pose_proj, preferred_element_type=jnp.float32
    )
    return guided.astype(jnp.bfloat16)


def attend_rows(queries, query_clip, query_block, keyvals, clip_of, block_ids):
    heads_dev = queries.shape[1]
    rows_query = queries.shape[0]
    head_size = queries.shape[2]
    score_scale = head_size ** (-0.5)
    start_carry = (
        jnp.full((heads_dev, rows_query), NEG_FILL, jnp.float32),
        jnp.zeros((heads_dev, rows_query), jnp.float32),
        jnp.zeros((heads_dev, rows_query, head_size), jnp.float32),
    )

    def one_frame(running, frame_item):
        frame_kv, frame_id = frame_item
        key_clip = clip_of[frame_id]
        key_block = block_ids[frame_id]
        visible = (query_clip == key_clip) & (key_block <= query_block)
        run_max, run_total, run_acc = running
        scores = (
            jnp.einsum(
                "qhd,khd->hqk", queries, frame_kv[:, :, 0], preferred_element_type=jnp.float32
            )
            * score_scale
        )
        scores = jnp.where(visible[None, :, None], scores, NEG_FILL)
        new_max = jnp.maximum(run_max, jnp.max(scores, axis=2))
        factor = jnp.exp(run_max - new_max)
        weights = jnp.where(visible[None, :, None], jnp.exp(scores - new_max[:, :, None]), 0.0)
        new_total = run_total * factor + jnp.sum(weights, axis=2)
        new_acc = run_acc * factor[:, :, None] + jnp.einsum(
            "hqk,khd->hqd",
            weights.astype(jnp.bfloat16),
            frame_kv[:, :, 1],
            preferred_element_type=jnp.float32,
        )
        running = (new_max, new_total, new_acc)
        return (running, None)

    running = start_carry
    shard_piece = lax.all_gather(keyvals, "frame", axis=0, tiled=True)
    piece_frames = shard_piece.shape[0]
    frame_list = jnp.arange(piece_frames, dtype=jnp.int32)
    running, unused = lax.scan(one_frame, running, (shard_piece, frame_list))
    run_max, run_total, run_acc = running
    normalized = run_acc / run_total[:, :, None]
    return jnp.transpose(normalized, (1, 0, 2)).astype(jnp.bfloat16)


def plain_shards(
    latent, pose_maps, conv_weight, conv_bias, pose_proj, w_qkv, w_out, clip_lengths, block_ids
):
    frame_count = block_ids.shape[0]
    clip_of, start_of = frame_tables(clip_lengths, frame_count)
    frames_dev = latent.shape[0]
    first_frame = lax.axis_index("frame") * frames_dev
    guided = guide_features(
        latent, pose_maps, conv_weight, conv_bias, pose_proj, start_of, first_frame
    )
    whole_rows = lax.all_gather(guided, "head", axis=1, tiled=True)
    height = whole_rows.shape[1]
    width_grid = whole_rows.shape[2]
    model_width = whole_rows.shape[3]
    flat_tokens = whole_rows.reshape(-1, model_width)
    qkv_local = w_qkv.reshape(w_qkv.shape[0], -1)
    projected = jnp.dot(
        flat_tokens,
        lax.all_gather(qkv_local, "frame", axis=0, tiled=True),
        preferred_element_type=jnp.float32,
    ).astype(jnp.bfloat16)
    per_frame = height * width_grid
    heads_dev = w_qkv.shape[1]
    head_size = w_qkv.shape[3]
    grouped = projected.reshape(frames_dev, per_frame, heads_dev, 3, head_size)
    rows_total = frames_dev * per_frame
    queries = grouped[:, :, :, 0].reshape(rows_total, heads_dev, head_size)
    keyvals = grouped[:, :, :, 1:3]
    clip_rows = lax.dynamic_slice_in_dim(clip_of, first_frame, frames_dev)
    block_rows = lax.dynamic_slice_in_dim(block_ids, first_frame, frames_dev)
    query_clip = jnp.repeat(clip_rows, per_frame)
    query_block = jnp.repeat(block_rows, per_frame)
    attended = attend_rows(queries, query_clip, query_block, keyvals, clip_of, block_ids)
    by_row = attended.reshape(frames_dev, height, width_grid, heads_dev * head_size)
    by_row = jnp.transpose(by_row, (1, 0, 2, 3)).reshape(
        height, frames_dev * width_grid, heads_dev * head_size
    )
    out_weight = w_out.reshape(heads_dev * head_size, w_out.shape[2])
    rows_here = height // lax.axis_size("head")
    summed_rows = lax.psum_scatter(
        jnp.dot(by_row, out_weight, preferred_element_type=jnp.float32).astype(jnp.bfloat16),
        "head",
        scatter_dimension=0,
        tiled=True,
    ).astype(jnp.float32)
    summed_rows = summed_rows.reshape(rows_here, frames_dev, width_grid, out_weight.shape[1])
    return jnp.transpose(summed_rows, (1, 0, 2, 3)).astype(jnp.bfloat16)


def turn(value, axis, steps):
    count = lax.axis_size(axis)
    return lax.ppermute(value, axis, [(i, (i + steps) % count) for i in range(count)])


def across(value, axis, bits):
    count = lax.axis_size(axis)
    return lax.ppermute(value, axis, [(i, i ^ bits) for i in range(count)])


def hop(lower, upper, axis, s):
    count = lax.axis_size(axis)
    lower = lax.ppermute(lower, axis, [(i, i + 1) for i in range(s - 1, count - 1)])
    upper = lax.ppermute(upper, axis, [(i, i - 1) for i in range(1, count - s + 1)])
    return lower, upper


def after(value, *others):
    def body(*refs):
        del refs

    anywhere = pl.BlockSpec(memory_space=pl.ANY)
    return pl.pallas_call(
        body,
        out_shape=jax.ShapeDtypeStruct(value.shape, value.dtype),
        in_specs=[anywhere] * (1 + len(others)),
        out_specs=anywhere,
        input_output_aliases={0: 0},
        name="after",
    )(value, *others)


def take_block(weight, row, column, shape, *ready):
    def body(at_ref, weight_ref, *refs):
        refs[-1][...] = weight_ref[...]

    return pl.pallas_call(
        body,
        out_shape=jax.ShapeDtypeStruct(shape, weight.dtype),
        grid_spec=pltpu.PrefetchScalarGridSpec(
            num_scalar_prefetch=1,
            grid=(1,),
            in_specs=[pl.BlockSpec(shape, lambda i, at: (at[0], at[1]))]
            + [pl.BlockSpec(memory_space=pl.ANY)] * len(ready),
            out_specs=pl.BlockSpec(shape, lambda i, at: (0, 0)),
        ),
        cost_estimate=cost(0, 4 * shape[0] * shape[1]),
        name="take_block",
    )(jnp.stack([row, column]), weight, *ready)


def conv_kernel(keep_ref, cols_ref, weight_ref, bias_ref, out_ref, acc_ref):
    step = pl.program_id(0)
    tap_a, tap_b = step // 3, step % 3
    frames, strip_rows, width = out_ref.shape[0], out_ref.shape[1], cols_ref.shape[2]
    pieces = []
    for t in range(frames):
        keep = keep_ref[tap_a * frames + t]
        for r in range(strip_rows):
            rows = cols_ref[tap_a + t, tap_b + 2 * r].astype(F32)
            pieces.append(jnp.where(keep > 0, rows, 0.0))
    lhs = jnp.concatenate(pieces, axis=0).astype(BF16)
    channels = weight_ref.shape[3]
    total = None
    for e in range(3):
        part = lax.dot_general(
            lhs[:, e * channels : (e + 1) * channels],
            weight_ref[0, e],
            (((1,), (1,)), ((), ())),
            preferred_element_type=F32,
        )
        total = part if total is None else total + part

    @pl.when(step == 0)
    def _():
        acc_ref[...] = total

    @pl.when(step > 0)
    def _():
        acc_ref[...] += total

    @pl.when(step == 8)
    def _():
        summed = acc_ref[...] + bias_ref[...]
        feature = summed / (1.0 + jnp.exp(-summed))
        for t in range(frames):
            for r in range(strip_rows):
                at = (t * strip_rows + r) * width
                out_ref[t, r] = feature[at : at + width].astype(BF16)


def pose_feature(extended, conv_weight, conv_bias, start_of, first_frame):
    frames, rows, columns, channels = extended.shape
    frames, rows = frames // 2, rows - 1
    out_channels = conv_weight.shape[-1]
    pairs = extended.reshape(2 * frames, rows + 1, columns // 2, 2 * channels)
    before = jnp.pad(pairs[:, :, :-1, channels:], ((0, 0), (0, 0), (1, 0), (0, 0)))
    cols = jnp.concatenate([before, pairs], axis=3)
    taps = jnp.transpose(conv_weight, (0, 1, 2, 4, 3)).reshape(9, 3, out_channels, channels)
    frame_ids = first_frame + jnp.arange(frames, dtype=jnp.int32)
    starts_here = lax.dynamic_slice_in_dim(start_of, first_frame, frames)
    keep = (frame_ids[None, :] - 2 + jnp.arange(3, dtype=jnp.int32)[:, None] >= starts_here[None, :])
    keep = keep.astype(jnp.int32).reshape(-1)
    out_shape = (frames, rows // 2, columns // 2, out_channels)
    tokens = frames * (rows // 2) * (columns // 2)
    feature = pl.pallas_call(
        conv_kernel,
        out_shape=jax.ShapeDtypeStruct(out_shape, BF16),
        grid_spec=pltpu.PrefetchScalarGridSpec(
            num_scalar_prefetch=1,
            grid=(9,),
            in_specs=[
                pl.BlockSpec(cols.shape, lambda i, k: (0, 0, 0, 0)),
                pl.BlockSpec((1, 3, out_channels, channels), lambda i, k: (i, 0, 0, 0)),
                pl.BlockSpec((1, out_channels), lambda i, k: (0, 0)),
            ],
            out_specs=pl.BlockSpec(out_shape, lambda i, k: (0, 0, 0, 0)),
            scratch_shapes=[pltpu.VMEM((tokens, out_channels), F32)],
        ),
        compiler_params=pltpu.CompilerParams(vmem_limit_bytes=24 * MIB),
        cost_estimate=cost(tokens * out_channels, 2 * tokens * out_channels),
        name="pose_conv",
    )(keep, cols, taps, conv_bias.reshape(1, -1))
    return feature.reshape(tokens, out_channels)


def guide(own, feature, pose_proj):
    tokens, width = own.shape
    channels = pose_proj.shape[0]
    wide = width // 4

    def body(own_ref, feature_ref, proj_ref, out_ref):
        added = jnp.dot(feature_ref[...], proj_ref[...], preferred_element_type=F32)
        out_ref[...] = (own_ref[...].astype(F32) + added).astype(BF16)

    return pl.pallas_call(
        body,
        out_shape=jax.ShapeDtypeStruct(own.shape, BF16),
        grid=(4,),
        in_specs=[
            pl.BlockSpec((tokens, wide), lambda i: (0, i)),
            pl.BlockSpec((tokens, channels), lambda i: (0, 0)),
            pl.BlockSpec((channels, wide), lambda i: (0, i)),
        ],
        out_specs=pl.BlockSpec((tokens, wide), lambda i: (0, i)),
        compiler_params=pltpu.CompilerParams(vmem_limit_bytes=16 * MIB),
        cost_estimate=cost(tokens * width, 2 * tokens * width),
        name="guide",
    )(own, feature, pose_proj)


def project(own, lower, upper, order, shards_of, total, frames):
    strips = len(lower) + 1
    tokens = own.shape[0]
    rows = strips * tokens
    per_frame = tokens // frames
    steps = len(shards_of)
    flat = [array for kind, arrays in shards_of for array in arrays]
    size = flat[0].shape[2]
    columns = 3 * (PLANE + 1)
    heads = PLANE + 1
    depth = own.shape[1] // PLANE
    cuts = [(c, min(c + 4, columns)) for c in range(0, columns, 4)]
    parts = 2 if shards_of[0][0] == "rows" else 1
    slots = min(2, steps)

    def body(order_ref, *refs):
        own_ref, lower_refs, upper_refs = refs[0], refs[1:strips], refs[strips : 2 * strips - 1]
        source_refs = refs[2 * strips - 1 : 2 * strips - 1 + len(flat)]
        rest = refs[2 * strips - 1 + len(flat) :]
        held_ref, guided_ref, sems = rest[-3:]
        if total is None:
            sum_ref = rest[0]
        else:
            total_ref, last_ref, sum_ref = rest[0], rest[1 + PLANE], rest[2 + PLANE]
            message_refs = rest[1 : 1 + PLANE]
        step = pl.program_id(0)

        def fetch(k, n, part):
            low, high = cuts[n]
            kind, arrays = shards_of[k]
            base = sum(len(other) for unused, other in shards_of[:k])
            length, at, shift = depth // parts, 0, 0
            if kind == "columns" and low >= FIRST_COLUMNS:
                base, shift = base + 1, FIRST_COLUMNS
            if kind == "rows":
                base += part
                at = pl.multiple_of((order_ref[steps + 1] ^ part) * length, 128)
            return pltpu.make_async_copy(
                source_refs[base].at[low - shift : high - shift],
                held_ref.at[k % slots, low:high, pl.ds(at, length)],
                sems.at[k % slots, n, part],
            )

        def start(k):
            for n in range(len(cuts)):
                for part in range(parts):
                    fetch(k, n, part).start()

        for k in range(steps):

            @pl.when(step == max(k - 1, 0))
            def _(k=k):
                start(k)

        for s in range(strips):
            found = own_ref[...]
            if s > 0:
                found = lower_refs[s - 1][...].astype(F32) + upper_refs[strips - s - 1][...].astype(F32)
                found = found.astype(BF16)
            for t in range(frames):
                at = (t * strips + s) * per_frame
                guided_ref[at : at + per_frame] = found[t * per_frame : (t + 1) * per_frame]

        slot = lax.rem(step, slots)
        for n, (low, high) in enumerate(cuts):
            for k in range(steps):

                @pl.when(step == k)
                def _(k=k, n=n):
                    for part in range(parts):
                        fetch(k, n, part).wait()

            rhs = jnp.concatenate([held_ref[slot, c] for c in range(low, high)], axis=1)
            part = jnp.dot(guided_ref[...], rhs, preferred_element_type=F32)
            lanes = slice(low * size, high * size)
            if total is not None:
                sum_ref[:, lanes] = total_ref[:, lanes] + part
                continue

            @pl.when(step == 0)
            def _(lanes=lanes, part=part):
                sum_ref[:, lanes] = part

            @pl.when(step > 0)
            def _(lanes=lanes, part=part):
                sum_ref[:, lanes] += part

        if total is None:
            return
        last = 3 * (heads - 1) * size
        last_ref[...] = sum_ref[:, last : last + size].astype(BF16)
        for r in range(PLANE):
            head = order_ref[steps] ^ r
            for j in range(3):
                at = pl.multiple_of((3 * head + j) * size, size)
                message_refs[r][j] = sum_ref[:, pl.ds(at, size)].astype(BF16)
            for j in range(1, 3):
                at = last + j * size
                message_refs[r][2 + j] = sum_ref[:, at : at + size].astype(BF16)

    piece = pl.BlockSpec((tokens, depth), lambda i, order: (0, order[i]))
    in_specs = [piece] * (2 * strips - 1)
    in_specs += [pl.BlockSpec(memory_space=pl.ANY)] * len(flat)
    operands = [own, *lower, *upper, *flat]
    sums = pl.BlockSpec((rows, columns * size), lambda i, order: (0, 0))
    scratch = [
        pltpu.VMEM((slots, columns, depth, size), BF16),
        pltpu.VMEM((rows, depth), BF16),
        pltpu.SemaphoreType.DMA((slots, len(cuts), parts)),
    ]
    if total is None:
        out_shape, out_specs = jax.ShapeDtypeStruct((rows, columns * size), F32), sums
    else:
        assert steps == 1
        in_specs.append(sums)
        operands.append(total)
        message = jax.ShapeDtypeStruct((5, rows, size), BF16)
        out_shape = (message,) * PLANE + (jax.ShapeDtypeStruct((rows, size), BF16),)
        out_specs = (pl.BlockSpec((5, rows, size), lambda i, order: (0, 0, 0)),) * PLANE
        out_specs += (pl.BlockSpec((rows, size), lambda i, order: (0, 0)),)
        scratch = [pltpu.VMEM((rows, columns * size), F32)] + scratch
    return pl.pallas_call(
        body,
        out_shape=out_shape,
        grid_spec=pltpu.PrefetchScalarGridSpec(
            num_scalar_prefetch=1, grid=(steps,), in_specs=in_specs, out_specs=out_specs, scratch_shapes=scratch
        ),
        compiler_params=pltpu.CompilerParams(vmem_limit_bytes=40 * MIB),
        cost_estimate=cost(0, 2 * rows * size),
        name="project",
    )(order, *operands)


def attend(messages, last_query, here, spans, frames, strips):
    rows, size = last_query.shape
    per_frame = rows // frames
    strip = per_frame // strips
    frame_count = PLANE * frames
    window = frame_count - 4 if frame_count > 4 else frame_count
    out_rows = (PLANE + 1) * frames * strip
    scale = size ** (-0.5)

    def body(table_ref, *refs):
        message_refs, last_ref = refs[:PLANE], refs[PLANE]
        out_refs, held_ref = refs[PLANE + 1 : PLANE + 1 + strips], refs[-1]
        here_at = table_ref[3 * frame_count]
        for r in range(PLANE):
            for t in range(frames):
                frame = (here_at ^ r) * frames + t
                for j in range(4):
                    held_ref[frame, j] = message_refs[r][j + 1, t * per_frame : (t + 1) * per_frame]

        def one(query, frame, kind, at):
            begin, low, high = table_ref[3 * frame], table_ref[3 * frame + 1], table_ref[3 * frame + 2]
            keys = held_ref[pl.ds(begin, window), kind].reshape(window * per_frame, size)
            values = held_ref[pl.ds(begin, window), kind + 1].reshape(window * per_frame, size)
            scores = lax.dot_general(query, keys, (((1,), (1,)), ((), ())), preferred_element_type=F32)
            place = lax.broadcasted_iota(jnp.int32, (1, window * per_frame), 1)
            seen = (place >= low * per_frame) & (place < high * per_frame)
            scores = jnp.where(seen, scores * scale, NEG_FILL)
            weights = jnp.exp(scores - jnp.max(scores, axis=1, keepdims=True))
            totals = jnp.sum(weights, axis=1, keepdims=True)
            mixed = jnp.dot(weights.astype(BF16), values, preferred_element_type=F32)
            result = (mixed / totals).astype(BF16)
            for s in range(strips):
                out_refs[s][at : at + strip] = result[s * strip : (s + 1) * strip]

        for r in range(PLANE):
            for t in range(frames):
                query = message_refs[r][0, t * per_frame : (t + 1) * per_frame]
                one(query, (here_at ^ r) * frames + t, 0, (r * frames + t) * strip)
        for t in range(frames):
            query = last_ref[t * per_frame : (t + 1) * per_frame]
            one(query, here_at * frames + t, 2, (PLANE * frames + t) * strip)

    table = jnp.concatenate([spans.reshape(-1), here.reshape(1)]).astype(jnp.int32)
    whole = pl.BlockSpec((5, rows, size), lambda i, table: (0, 0, 0))
    units = (PLANE + 1) * frames
    return pl.pallas_call(
        body,
        out_shape=(jax.ShapeDtypeStruct((out_rows, size), BF16),) * strips,
        grid_spec=pltpu.PrefetchScalarGridSpec(
            num_scalar_prefetch=1,
            grid=(1,),
            in_specs=[whole] * PLANE + [pl.BlockSpec((rows, size), lambda i, table: (0, 0))],
            out_specs=(pl.BlockSpec((out_rows, size), lambda i, table: (0, 0)),) * strips,
            scratch_shapes=[pltpu.VMEM((frame_count, 4, per_frame, size), BF16)],
        ),
        compiler_params=pltpu.CompilerParams(vmem_limit_bytes=40 * MIB),
        cost_estimate=cost(0, 2 * rows * size),
        name="attend",
    )(table, *messages, last_query)


def out_project(gathered, weights, here, group, core, tokens):
    groups, depth, columns = weights[0].shape
    size = gathered[0].shape[2]
    heads = depth // size

    def body(at_ref, *refs):
        weight_refs = refs[PLANE : PLANE + 2]
        out_refs, lhs_ref, sum_ref = refs[PLANE + 2 : -2], refs[-2], refs[-1]
        step = pl.program_id(0)
        for p in range(PLANE):
            rows = slice(p * tokens, (p + 1) * tokens)
            for q in range(PLANE):
                at = (p ^ q) * tokens
                lhs_ref[rows, q * size : (q + 1) * size] = refs[q][0, at : at + tokens]
            lhs_ref[rows, PLANE * size :] = refs[p][0, PLANE * tokens :]

        here_at, core_at = at_ref[0], at_ref[2]
        for c in range(2):
            found = [
                weight_refs[c][0, pl.ds(pl.multiple_of((here_at ^ q) * size, size), size)] for q in range(PLANE)
            ]
            found.append(weight_refs[c][0, PLANE * size : heads * size])
            part = jnp.dot(lhs_ref[...], jnp.concatenate(found, axis=0), preferred_element_type=F32)
            part = part.astype(BF16).astype(F32)

            @pl.when(step == 0)
            def _(c=c, part=part):
                sum_ref[c] = part

            @pl.when(step > 0)
            def _(c=c, part=part):
                sum_ref[c] += part

        @pl.when(step == groups - 1)
        def _():
            for p in range(PLANE):
                for c in range(2):
                    at = pl.multiple_of((core_at ^ c) * columns, 128)
                    out_refs[p][:, pl.ds(at, columns)] = sum_ref[c, p * tokens : (p + 1) * tokens].astype(BF16)

    in_specs = [pl.BlockSpec((1,) + piece.shape[1:], lambda g, at: (g, 0, 0)) for piece in gathered]
    in_specs += [
        pl.BlockSpec((1, depth, columns), lambda g, at: (lax.rem(at[1] + g, groups), 0, 0))
    ] * 2
    return pl.pallas_call(
        body,
        out_shape=(jax.ShapeDtypeStruct((tokens, 2 * columns), BF16),) * PLANE,
        grid_spec=pltpu.PrefetchScalarGridSpec(
            num_scalar_prefetch=1,
            grid=(groups,),
            in_specs=in_specs,
            out_specs=(pl.BlockSpec((tokens, 2 * columns), lambda g, at: (0, 0)),) * PLANE,
            scratch_shapes=[
                pltpu.VMEM((PLANE * tokens, depth), BF16),
                pltpu.VMEM((2, PLANE * tokens, columns), F32),
            ],
        ),
        compiler_params=pltpu.CompilerParams(vmem_limit_bytes=24 * MIB),
        cost_estimate=cost(0, 4 * PLANE * tokens * columns),
        name="out_project",
    )(jnp.stack([here, group, core]), *gathered, *weights)


def place_columns(pieces, here):
    tokens, columns = pieces[0].shape

    def body(here_ref, *refs):
        for r in range(PLANE):
            at = pl.multiple_of((here_ref[0] ^ r) * columns, 128)
            refs[-1][:, pl.ds(at, columns)] = refs[r][...]

    return pl.pallas_call(
        body,
        out_shape=jax.ShapeDtypeStruct((tokens, PLANE * columns), BF16),
        grid_spec=pltpu.PrefetchScalarGridSpec(
            num_scalar_prefetch=1,
            grid=(1,),
            in_specs=[pl.BlockSpec((tokens, columns), lambda i, here: (0, 0))] * PLANE,
            out_specs=pl.BlockSpec((tokens, PLANE * columns), lambda i, here: (0, 0)),
        ),
        cost_estimate=cost(0, 4 * tokens * PLANE * columns),
        name="place_columns",
    )(here.reshape(1), *pieces)


def shards(
    latent, pose_maps, conv_weight, conv_bias, pose_proj, w_qkv, w_out, clip_lengths, block_ids
):
    frame_count = block_ids.shape[0]
    frames, strip_rows, width_grid, model_width = latent.shape
    heads, head_size = w_qkv.shape[1], w_qkv.shape[3]
    strips = lax.axis_size("head")
    tokens = frames * strip_rows * width_grid
    here = lax.axis_index("frame").astype(jnp.int32)
    group = lax.axis_index("head").astype(jnp.int32)
    core = lax.axis_index("dp").astype(jnp.int32)
    clip_of, start_of = frame_tables(clip_lengths, frame_count)

    weight = jnp.transpose(w_qkv, (1, 2, 0, 3)).reshape(3 * heads, -1, head_size)
    near_pairs = [(2 * f + c, 2 * (f ^ (1 + c)) + c) for f in range(PLANE) for c in range(2)]
    far_pairs = [(2 * f + c, 2 * (f ^ (2 - c)) + c) for f in range(PLANE) for c in range(2)]
    plane_axes = ("frame", "dp")
    earlier = shifted(pose_maps, "frame", 1)
    near_first = lax.ppermute(after(weight[:FIRST_COLUMNS], earlier), plane_axes, near_pairs)
    extended = jnp.concatenate([earlier, pose_maps], axis=0)
    extended = jnp.concatenate([shifted(extended[:, -1:], "head", 1), extended], axis=1)
    feature = pose_feature(extended, conv_weight, conv_bias, start_of, here * frames)
    own = guide(latent.reshape(tokens, model_width), feature, pose_proj)
    near_rest = lax.ppermute(after(weight[FIRST_COLUMNS:], own), plane_axes, near_pairs)
    lower, upper = hop(own, own, "head", 1)
    lower, upper = [lower], [upper]
    columns = model_width // PLANE // 2
    depth = heads * head_size
    out_half = take_block(w_out.reshape(depth, model_width), jnp.int32(0), 2 * here + core, (depth, columns))

    half_rows = weight.shape[1] // 2
    near = (near_first, after(near_rest, lower[0], upper[0], out_half))
    passed = jnp.concatenate(
        [lax.dynamic_slice_in_dim(part, core * half_rows, half_rows, axis=1) for part in near], axis=0
    )
    far = lax.ppermute(passed, plane_axes, far_pairs)
    for s in range(2, strips):
        below, above = hop(lower[-1], upper[-1], "head", s)
        if s < strips - 1:
            below, above = after(below, passed), after(above, passed)
        lower.append(below)
        upper.append(above)
    other = tuple(across(part, "dp", 1) for part in near)
    out_half = after(out_half, lower[-1], upper[-1])

    here_near, here_other, here_far = here ^ (1 + core), here ^ (2 - core), here ^ 3
    order = after(jnp.stack([here, here_near, here_other, here, core]), out_half)
    held = [("whole", (weight,)), ("columns", near), ("columns", other)]
    total = project(own, lower, upper, order, held, None, frames)
    far = (far, across(far, "dp", 1))
    order = jnp.stack([here_far, here, core])
    *messages, last_query = project(
        own, lower, upper, order, [("rows", far)], total, frames
    )
    messages = [messages[0]] + [across(messages[r], "frame", r) for r in range(1, PLANE)]

    same_clip = clip_of[:, None] == clip_of[None, :]
    counts = jnp.sum((same_clip & (block_ids[None, :] <= block_ids[:, None])).astype(jnp.int32), axis=1)
    window = frame_count - 4 if frame_count > 4 else frame_count
    begins = jnp.minimum(start_of, frame_count - window)
    spans = jnp.stack([begins, start_of - begins, start_of - begins + counts], axis=1)
    outs = attend(messages, last_query, here, spans, frames, strips)

    out_half = after(lax.all_gather(out_half, "head"), outs[0])
    out_weights = [out_half, across(out_half, "dp", 1)]

    strip_heads = [outs[0]] + [turn(outs[s], "head", -s) for s in range(1, strips)]
    strip_heads = after(jnp.stack(strip_heads), out_weights[1])
    gathered = [strip_heads] + [across(strip_heads, "frame", r) for r in range(1, PLANE)]
    done = out_project(gathered, out_weights, here, group, core, tokens)
    mine = [done[0]] + [across(done[r], "frame", r) for r in range(1, PLANE)]
    return place_columns(mine, here).reshape(latent.shape)


def solution(mesh):
    return jax.shard_map(
        shards if mesh.shape["frame"] == PLANE else plain_shards,
        mesh=mesh,
        in_specs=(
            P(("dp", "frame"), "head", None, None),
            P(("dp", "frame"), "head", None, None),
            P(),
            P(),
            P(),
            P("frame", "head", None, None),
            P("head", None, None),
            P("dp"),
            P("dp"),
        ),
        out_specs=P(("dp", "frame"), "head", None, None),
        check_vma=False,
    )
```

profile of v0, /device:TPU:0, one launch (start us, length us, event | category | flops | bytes accessed | tf_op | source)
XLA Modules:
  0.0 259.8 jit_solution(8867922591115893277)
XLA Ops:
  6.5 4.8 %collective-permute-start = (bf16[2,4,48,256]{3,2,1,0:T(8,128)(2,1)}, bf16[2,4,48,256]{3,2,1,0:T(8,128)(2,1)S(1)}, u32[]{:S(2)}, u32[]{:S(2)}) collective-permute-start(bf16[2,4,48,256]{3,2,1,0:T(8,128)(2,1)} %param.10), channel_id=1, source_target_pairs={{0,8},{8,16},{16,24},{1,9},{9,17},{17,25},{2,10},{10,18},{18,26},{... | collective-permute-start | bytes 589832 | tf_op jit(solution)/shard_map/ppermute | solution.py:23
  13.1 2.7 %collective-permute-done.refs_1_ = bf16[2,4,48,256]{3,2,1,0:T(8,128)(2,1)S(1)} collective-permute-done((bf16[2,4,48,256]{3,2,1,0:T(8,128)(2,1)}, bf16[2,4,48,256]{3,2,1,0:T(8,128)(2,1)S(1)}, u32[]{:S(2)}, u32[]{:S(2)}) %collective-permute-start) | collective-permute-done | bytes 196640 | tf_op jit(solution)/shard_map/ppermute | solution.py:23
  17.0 3.6 %collective-permute-start.1 = (bf16[4,1,48,256]{3,2,1,0:T(8,128)(2,1)S(1)}, bf16[4,1,48,256]{3,2,1,0:T(8,128)(2,1)S(1)}, u32[]{:S(2)}, u32[]{:S(2)}) collective-permute-start(bf16[4,1,48,256]{3,2,1,0:T(8,128)(2,1)S(1)} %slice.16), channel_id=1, source_target_pairs={{0,2},{2,4},{4,6},{1,3},{3,5},{5,7},{8,10},{10,12},{12,14},{9,11},... | collective-permute-start | bytes 294920 | tf_op jit(solution)/shard_map/ppermute | solution.py:23
  20.6 3.3 %slice.19.refs_0_ = bf16[7,1280,128]{2,1,0:T(8,128)(2,1)} slice(bf16[15,1280,128]{2,1,0:T(8,128)(2,1)} %bitcast.41), slice={[8:15], [0:1280], [0:128]} | slice | bytes 4587520 | tf_op jit(solution)/shard_map/slice | solution.py:622
  25.6 2.4 collective-permute-start.4
  28.4 2.2 copy-done.7
  30.7 3.4 %pose_conv.1 = bf16[2,2,24,320]{3,2,1,0:T(8,128)(2,1)S(1)} custom-call(s32[6]{0:T(128)S(1)} %reshape.111.keep_ref, bf16[4,5,24,768]{3,2,1,0:T(8,128)(2,1)S(1)} %fusion.1.cols_ref, bf16[9,3,320,256]{3,2,1,0:T(8,128)(2,1)S(1)} %bitcast.37, f32[1,320]{1,0:T(1,128)S(1)} %reshape.106.bias_ref), custom_call_target="tpu_custom_call" | custom-call | flops 30720 | bytes 61440 | tf_op jit(solution)/shard_map/pose_conv/pallas_call | solution.py:274
  38.0 5.5 %collective-permute-start.2 = (bf16[96,5120]{1,0:T(8,128)(2,1)}, bf16[96,5120]{1,0:T(8,128)(2,1)}, u32[]{:S(2)}, u32[]{:S(2)}) collective-permute-start(bf16[96,5120]{1,0:T(8,128)(2,1)} %copy-done), channel_id=1, source_target_pairs={{0,2},{2,4},{4,6},{1,3},{3,5},{5,7},{8,10},{10,12},{12,14},{9,11},... | collective-permute-start | bytes 2949128 | tf_op jit(solution)/shard_map/ppermute | solution.py:181
  43.6 18.3 %collective-permute-done.6.refs_2_.refs_4_ = bf16[96,5120]{1,0:T(8,128)(2,1)S(1)} collective-permute-done((bf16[96,5120]{1,0:T(8,128)(2,1)}, bf16[96,5120]{1,0:T(8,128)(2,1)S(1)}, u32[]{:S(2)}, u32[]{:S(2)}) %collective-permute-start.6) | collective-permute-done | bytes 983072 | tf_op jit(solution)/shard_map/ppermute | solution.py:182
  65.3 2.8 %take_block.1.refs_3_.refs_0_ = bf16[640,640]{1,0:T(8,128)(2,1)} custom-call(s32[2]{0:T(128)} %pad_add_fusion.2.at_ref, bf16[640,5120]{1,0:T(8,128)(2,1)} %bitcast.44), custom_call_target="tpu_custom_call" | custom-call | bytes 1638400 | tf_op jit(solution)/shard_map/take_block/pallas_call | solution.py:205
  68.2 14.3 %collective-permute-done.5.refs_0_ = bf16[7,1280,128]{2,1,0:T(8,128)(2,1)S(1)} collective-permute-done((bf16[7,1280,128]{2,1,0:T(8,128)(2,1)}, bf16[7,1280,128]{2,1,0:T(8,128)(2,1)S(1)}, u32[]{:S(2)}, u32[]{:S(2)}) %collective-permute-start.5) | collective-permute-done | bytes 2293792 | tf_op jit(solution)/shard_map/ppermute | solution.py:622
  89.7 1.8 collective-permute-start.7
  91.5 2.9 %collective-permute-start.10 = (bf16[15,640,128]{2,1,0:T(8,128)(2,1)}, bf16[15,640,128]{2,1,0:T(8,128)(2,1)}, u32[]{:S(2)}, u32[]{:S(2)}) collective-permute-start(bf16[15,640,128]{2,1,0:T(8,128)(2,1)} %pad_maximum_fusion.refs_1_), channel_id=1, source_target_pairs={{0,16},{1,9},{8,24},{9,1},{16,0},{17,25},{24,8},{25,17},{2,18},{3,... | collective-permute-start | bytes 7372808 | tf_op jit(solution)/shard_map/ppermute | solution.py:634
  94.4 18.9 %collective-permute-done.9.refs_2_.refs_6_ = bf16[96,5120]{1,0:T(8,128)(2,1)} collective-permute-done((bf16[96,5120]{1,0:T(8,128)(2,1)}, bf16[96,5120]{1,0:T(8,128)(2,1)}, u32[]{:S(2)}, u32[]{:S(2)}) %collective-permute-start.9) | collective-permute-done | bytes 983072 | tf_op jit(solution)/shard_map/ppermute | solution.py:182
  113.4 9.1 %collective-permute-done.10.refs_7_ = bf16[15,640,128]{2,1,0:T(8,128)(2,1)} collective-permute-done((bf16[15,640,128]{2,1,0:T(8,128)(2,1)}, bf16[15,640,128]{2,1,0:T(8,128)(2,1)}, u32[]{:S(2)}, u32[]{:S(2)}) %collective-permute-start.10) | collective-permute-done | bytes 2457632 | tf_op jit(solution)/shard_map/ppermute | solution.py:634
  123.8 6.7 %collective-permute-done.13.refs_11_ = bf16[7,1280,128]{2,1,0:T(8,128)(2,1)} collective-permute-done((bf16[7,1280,128]{2,1,0:T(8,128)(2,1)S(1)}, bf16[7,1280,128]{2,1,0:T(8,128)(2,1)}, u32[]{:S(2)}, u32[]{:S(2)}) %collective-permute-start.13) | collective-permute-done | bytes 2293792 | tf_op jit(solution)/shard_map/ppermute | solution.py:176
  132.4 14.5 %project.2.refs_9_ = f32[384,1920]{1,0:T(8,128)} custom-call(s32[5]{0:T(128)S(1)} %copy-done.14, bf16[96,5120]{1,0:T(8,128)(2,1)S(1)} %copy-done.1, bf16[96,5120]{1,0:T(8,128)(2,1)} %collective-permute-done.2.refs_1_, bf16[96,5120]{1,0:T(8,128)(2,1)} %after.12.refs_2_, bf16[96,5120]{1,0:T(8,128)(2,1)} %collective-permute-done.7.refs_1_.refs_3_, ...), custom_call_target="tpu_custom_call" | custom-call | bytes 98304 | tf_op jit(solution)/shard_map/project/pallas_call | solution.py:441
  146.9 7.9 %project.3 = (bf16[5,384,128]{2,1,0:T(8,128)(2,1)S(1)}, bf16[5,384,128]{2,1,0:T(8,128)(2,1)}, bf16[5,384,128]{2,1,0:T(8,128)(2,1)S(1)}, bf16[5,384,128]{2,1,0:T(8,128)(2,1)S(1)}, bf16[384,128]{1,0:T(8,128)(2,1)S(1)}) custom-call(s32[3]{0:T(128)S(1)} %add_add_fusion.1.order_ref, bf16[96,5120]{1,0:T(8,128)(2,1)S(1)} %copy-done.1, ...), custom_call_target="tpu_custom_call" | custom-call | bytes 98304 | tf_op jit(solution)/shard_map/project/pallas_call | solution.py:441
  158.9 10.3 %collective-permute-done.14.refs_1_ = bf16[5,384,128]{2,1,0:T(8,128)(2,1)S(1)} collective-permute-done((bf16[5,384,128]{2,1,0:T(8,128)(2,1)}, bf16[5,384,128]{2,1,0:T(8,128)(2,1)S(1)}, u32[]{:S(2)}, u32[]{:S(2)}) %collective-permute-start.14) | collective-permute-done | bytes 491552 | tf_op jit(solution)/shard_map/ppermute | solution.py:176
  169.2 9.4 %collective-permute-done.15.refs_2_ = bf16[5,384,128]{2,1,0:T(8,128)(2,1)S(1)} collective-permute-done((bf16[5,384,128]{2,1,0:T(8,128)(2,1)S(1)}, bf16[5,384,128]{2,1,0:T(8,128)(2,1)S(1)}, u32[]{:S(2)}, u32[]{:S(2)}) %collective-permute-start.15) | collective-permute-done | bytes 491552 | tf_op jit(solution)/shard_map/ppermute | solution.py:176
  178.6 1.8 collective-permute-done.16.refs_3_
  180.4 4.3 %attend.1 = (bf16[480,128]{1,0:T(8,128)(2,1)S(1)}, bf16[480,128]{1,0:T(8,128)(2,1)S(1)}, bf16[480,128]{1,0:T(8,128)(2,1)S(1)}, bf16[480,128]{1,0:T(8,128)(2,1)S(1)}) custom-call(s32[25]{0:T(128)S(1)} %pad_add_fusion.1.table_ref, bf16[5,384,128]{2,1,0:T(8,128)(2,1)S(1)} %get-tuple-element.18.refs_0_, ...), custom_call_target="tpu_custom_call" | custom-call | bytes 98304 | tf_op jit(solution)/shard_map/attend/pallas_call | solution.py:498
  185.5 1.8 collective-permute-start.17
  187.2 3.3 %collective-permute-start.18 = (bf16[480,128]{1,0:T(8,128)(2,1)S(1)}, bf16[480,128]{1,0:T(8,128)(2,1)S(1)}, u32[]{:S(2)}, u32[]{:S(2)}) collective-permute-start(bf16[480,128]{1,0:T(8,128)(2,1)S(1)} %get-tuple-element.25), channel_id=1, source_target_pairs={{0,4},{2,6},{4,0},{6,2},{1,5},{3,7},{5,1},{7,3},{8,12},{10,14},{12... | collective-permute-start | bytes 368648 | tf_op jit(solution)/shard_map/ppermute | solution.py:171
  191.3 1.8 collective-permute-done.17
  193.0 9.1 %collective-permute-done.18 = bf16[480,128]{1,0:T(8,128)(2,1)S(1)} collective-permute-done((bf16[480,128]{1,0:T(8,128)(2,1)S(1)}, bf16[480,128]{1,0:T(8,128)(2,1)S(1)}, u32[]{:S(2)}, u32[]{:S(2)}) %collective-permute-start.18) | collective-permute-done | bytes 122912 | tf_op jit(solution)/shard_map/ppermute | solution.py:171
  206.5 10.9 %collective-permute-done.21.refs_1_ = bf16[4,480,128]{2,1,0:T(8,128)(2,1)} collective-permute-done((bf16[4,480,128]{2,1,0:T(8,128)(2,1)}, bf16[4,480,128]{2,1,0:T(8,128)(2,1)}, u32[]{:S(2)}, u32[]{:S(2)}) %collective-permute-start.21) | collective-permute-done | bytes 491552 | tf_op jit(solution)/shard_map/ppermute | solution.py:176
  217.4 9.4 %collective-permute-done.22.refs_2_ = bf16[4,480,128]{2,1,0:T(8,128)(2,1)} collective-permute-done((bf16[4,480,128]{2,1,0:T(8,128)(2,1)}, bf16[4,480,128]{2,1,0:T(8,128)(2,1)}, u32[]{:S(2)}, u32[]{:S(2)}) %collective-permute-start.22) | collective-permute-done | bytes 491552 | tf_op jit(solution)/shard_map/ppermute | solution.py:176
  227.9 8.3 %out_project.1 = (bf16[96,1280]{1,0:T(8,128)(2,1)S(1)}, bf16[96,1280]{1,0:T(8,128)(2,1)S(1)}, bf16[96,1280]{1,0:T(8,128)(2,1)S(1)}, bf16[96,1280]{1,0:T(8,128)(2,1)S(1)}) custom-call(s32[3]{0:T(128)S(1)} %add_add_fusion.at_ref, bf16[4,480,128]{2,1,0:T(8,128)(2,1)S(1)} %copy-done.8, bf16[4,480,128]{2,1,0:T(8,128)(2,1)} %collective-permute-done.21.refs_1_, ...), custom_call_target="tpu_custom_call" | custom-call | bytes 983040 | tf_op jit(solution)/shard_map/out_project/pallas_call | solution.py:558
  240.4 5.4 %collective-permute-done.24.refs_1_ = bf16[96,1280]{1,0:T(8,128)(2,1)S(1)} collective-permute-done((bf16[96,1280]{1,0:T(8,128)(2,1)S(1)}, bf16[96,1280]{1,0:T(8,128)(2,1)S(1)}, u32[]{:S(2)}, u32[]{:S(2)}) %collective-permute-start.24) | collective-permute-done | bytes 245792 | tf_op jit(solution)/shard_map/ppermute | solution.py:176
  245.8 4.1 %collective-permute-done.25.refs_2_ = bf16[96,1280]{1,0:T(8,128)(2,1)S(1)} collective-permute-done((bf16[96,1280]{1,0:T(8,128)(2,1)S(1)}, bf16[96,1280]{1,0:T(8,128)(2,1)S(1)}, u32[]{:S(2)}, u32[]{:S(2)}) %collective-permute-start.25) | collective-permute-done | bytes 245792 | tf_op jit(solution)/shard_map/ppermute | solution.py:176
  250.7 2.3 place_columns.1
  (118 shorter events, 38.5 us)
Async XLA Ops:
  6.5 178.9 %all-gather.3.cloned.1.call-start = ((), (), s32[]{:S(2)}) async-start(), calls=%async_computation | async-start | bytes 4096000 | tf_op jit(solution)/shard_map/all_gather | solution.py:662
  6.5 9.3 %collective-permute-start = (bf16[2,4,48,256]{3,2,1,0:T(8,128)(2,1)}, bf16[2,4,48,256]{3,2,1,0:T(8,128)(2,1)S(1)}, u32[]{:S(2)}, u32[]{:S(2)}) collective-permute-start(bf16[2,4,48,256]{3,2,1,0:T(8,128)(2,1)} %param.10), channel_id=1, source_target_pairs={{0,8},{8,16},{16,24},{1,9},{9,17},{17,25},{2,10},{10,18},{18,26},{... | collective-permute-start | bytes 589832 | tf_op jit(solution)/shard_map/ppermute | solution.py:23
  17.0 11.1 %collective-permute-start.1 = (bf16[4,1,48,256]{3,2,1,0:T(8,128)(2,1)S(1)}, bf16[4,1,48,256]{3,2,1,0:T(8,128)(2,1)S(1)}, u32[]{:S(2)}, u32[]{:S(2)}) collective-permute-start(bf16[4,1,48,256]{3,2,1,0:T(8,128)(2,1)S(1)} %slice.16), channel_id=1, source_target_pairs={{0,2},{2,4},{4,6},{1,3},{3,5},{5,7},{8,10},{10,12},{12,14},{9,11},... | collective-permute-start | bytes 294920 | tf_op jit(solution)/shard_map/ppermute | solution.py:23
  25.6 59.6 %collective-permute-start.4 = (bf16[8,1280,128]{2,1,0:T(8,128)(2,1)}, bf16[8,1280,128]{2,1,0:T(8,128)(2,1)}, u32[]{:S(2)}, u32[]{:S(2)}) collective-permute-start(bf16[8,1280,128]{2,1,0:T(8,128)(2,1)} %after.9), channel_id=1, source_target_pairs={{0,8},{1,17},{8,0},{9,25},{16,24},{17,1},{24,16},{25,9},{2,10},{3,... | collective-permute-start | bytes 7864328 | tf_op jit(solution)/shard_map/ppermute | solution.py:617
  36.7 45.8 %collective-permute-start.5 = (bf16[7,1280,128]{2,1,0:T(8,128)(2,1)}, bf16[7,1280,128]{2,1,0:T(8,128)(2,1)S(1)}, u32[]{:S(2)}, u32[]{:S(2)}) collective-permute-start(bf16[7,1280,128]{2,1,0:T(8,128)(2,1)} %after.10), channel_id=1, source_target_pairs={{0,8},{1,17},{8,0},{9,25},{16,24},{17,1},{24,16},{25,9},{2,10},{3,... | collective-permute-start | bytes 6881288 | tf_op jit(solution)/shard_map/ppermute | solution.py:622
  36.7 25.1 %collective-permute-start.6 = (bf16[96,5120]{1,0:T(8,128)(2,1)}, bf16[96,5120]{1,0:T(8,128)(2,1)S(1)}, u32[]{:S(2)}, u32[]{:S(2)}) collective-permute-start(bf16[96,5120]{1,0:T(8,128)(2,1)} %copy-done), channel_id=1, source_target_pairs={{2,0},{4,2},{6,4},{3,1},{5,3},{7,5},{10,8},{12,10},{14,12},{11,9},... | collective-permute-start | bytes 2949128 | tf_op jit(solution)/shard_map/ppermute | solution.py:182
  38.0 25.1 %collective-permute-start.2 = (bf16[96,5120]{1,0:T(8,128)(2,1)}, bf16[96,5120]{1,0:T(8,128)(2,1)}, u32[]{:S(2)}, u32[]{:S(2)}) collective-permute-start(bf16[96,5120]{1,0:T(8,128)(2,1)} %copy-done), channel_id=1, source_target_pairs={{0,2},{2,4},{4,6},{1,3},{3,5},{5,7},{8,10},{10,12},{12,14},{9,11},... | collective-permute-start | bytes 2949128 | tf_op jit(solution)/shard_map/ppermute | solution.py:181
  61.8 26.5 %collective-permute-start.8 = (bf16[96,5120]{1,0:T(8,128)(2,1)S(1)}, bf16[96,5120]{1,0:T(8,128)(2,1)}, u32[]{:S(2)}, u32[]{:S(2)}) collective-permute-start(bf16[96,5120]{1,0:T(8,128)(2,1)S(1)} %collective-permute-done.6.refs_2_.refs_4_), channel_id=1, source_target_pairs={{2,0},{4,2},{3,1},{5,3},{10,8},{12,10},{11,9},{13,11},{18,16},{20,... | collective-permute-start | bytes 2949128 | tf_op jit(solution)/shard_map/ppermute | solution.py:182
  63.1 26.5 %collective-permute-start.3 = (bf16[96,5120]{1,0:T(8,128)(2,1)}, bf16[96,5120]{1,0:T(8,128)(2,1)}, u32[]{:S(2)}, u32[]{:S(2)}) collective-permute-start(bf16[96,5120]{1,0:T(8,128)(2,1)} %collective-permute-done.2.refs_1_), channel_id=1, source_target_pairs={{2,4},{4,6},{3,5},{5,7},{10,12},{12,14},{11,13},{13,15},{18,20},{2... | collective-permute-start | bytes 2949128 | tf_op jit(solution)/shard_map/ppermute | solution.py:181
  88.3 25.0 %collective-permute-start.9 = (bf16[96,5120]{1,0:T(8,128)(2,1)}, bf16[96,5120]{1,0:T(8,128)(2,1)}, u32[]{:S(2)}, u32[]{:S(2)}) collective-permute-start(bf16[96,5120]{1,0:T(8,128)(2,1)} %after.13.refs_5_), channel_id=1, source_target_pairs={{2,0},{3,1},{10,8},{11,9},{18,16},{19,17},{26,24},{27,25}} | collective-permute-start | bytes 2949128 | tf_op jit(solution)/shard_map/ppermute | solution.py:182
  89.6 33.0 %copy-start.3 = (bf16[7,1280,128]{2,1,0:T(8,128)(2,1)S(1)}, bf16[7,1280,128]{2,1,0:T(8,128)(2,1)}, u32[]{:S(2)}) copy-start(bf16[7,1280,128]{2,1,0:T(8,128)(2,1)} %after.11.refs_9_) | copy-start | bytes 6881284
  89.7 40.9 %copy-start.1 = (bf16[96,5120]{1,0:T(8,128)(2,1)S(1)}, bf16[96,5120]{1,0:T(8,128)(2,1)}, u32[]{:S(2)}) copy-start(bf16[96,5120]{1,0:T(8,128)(2,1)} %copy-done) | copy-start | bytes 2949124
  89.7 23.7 %collective-permute-start.7 = (bf16[96,5120]{1,0:T(8,128)(2,1)}, bf16[96,5120]{1,0:T(8,128)(2,1)}, u32[]{:S(2)}, u32[]{:S(2)}) collective-permute-start(bf16[96,5120]{1,0:T(8,128)(2,1)} %after.12.refs_2_), channel_id=1, source_target_pairs={{4,6},{5,7},{12,14},{13,15},{20,22},{21,23},{28,30},{29,31}} | collective-permute-start | bytes 2949128 | tf_op jit(solution)/shard_map/ppermute | solution.py:181
  91.5 31.1 %collective-permute-start.10 = (bf16[15,640,128]{2,1,0:T(8,128)(2,1)}, bf16[15,640,128]{2,1,0:T(8,128)(2,1)}, u32[]{:S(2)}, u32[]{:S(2)}) collective-permute-start(bf16[15,640,128]{2,1,0:T(8,128)(2,1)} %pad_maximum_fusion.refs_1_), channel_id=1, source_target_pairs={{0,16},{1,9},{8,24},{9,1},{16,0},{17,25},{24,8},{25,17},{2,18},{3,... | collective-permute-start | bytes 7372808 | tf_op jit(solution)/shard_map/ppermute | solution.py:634
  113.4 17.1 %collective-permute-start.12 = (bf16[8,1280,128]{2,1,0:T(8,128)(2,1)}, bf16[8,1280,128]{2,1,0:T(8,128)(2,1)}, u32[]{:S(2)}, u32[]{:S(2)}) collective-permute-start(bf16[8,1280,128]{2,1,0:T(8,128)(2,1)} %collective-permute-done.4.refs_8_), channel_id=1, source_target_pairs={{0,1},{1,0},{2,3},{3,2},{4,5},{5,4},{6,7},{7,6},{8,9},{9,8},{10,11... | collective-permute-start | bytes 7864328 | tf_op jit(solution)/shard_map/ppermute | solution.py:176
  122.6 24.3 %collective-permute-start.11 = (bf16[15,640,128]{2,1,0:T(8,128)(2,1)}, bf16[15,640,128]{2,1,0:T(8,128)(2,1)}, u32[]{:S(2)}, u32[]{:S(2)}) collective-permute-start(bf16[15,640,128]{2,1,0:T(8,128)(2,1)} %collective-permute-done.10.refs_7_), channel_id=1, source_target_pairs={{0,1},{1,0},{2,3},{3,2},{4,5},{5,4},{6,7},{7,6},{8,9},{9,8},{10,11... | collective-permute-start | bytes 7372808 | tf_op jit(solution)/shard_map/ppermute | solution.py:176
  122.6 7.9 %collective-permute-start.13 = (bf16[7,1280,128]{2,1,0:T(8,128)(2,1)S(1)}, bf16[7,1280,128]{2,1,0:T(8,128)(2,1)}, u32[]{:S(2)}, u32[]{:S(2)}) collective-permute-start(bf16[7,1280,128]{2,1,0:T(8,128)(2,1)S(1)} %copy-done.3), channel_id=1, source_target_pairs={{0,1},{1,0},{2,3},{3,2},{4,5},{5,4},{6,7},{7,6},{8,9},{9,8},{10,11... | collective-permute-start | bytes 6881288 | tf_op jit(solution)/shard_map/ppermute | solution.py:176
  154.9 14.3 %collective-permute-start.14 = (bf16[5,384,128]{2,1,0:T(8,128)(2,1)}, bf16[5,384,128]{2,1,0:T(8,128)(2,1)S(1)}, u32[]{:S(2)}, u32[]{:S(2)}) collective-permute-start(bf16[5,384,128]{2,1,0:T(8,128)(2,1)} %get-tuple-element.19), channel_id=1, source_target_pairs={{0,8},{8,0},{16,24},{24,16},{1,9},{9,1},{17,25},{25,17},{2,10},{10... | collective-permute-start | bytes 1474568 | tf_op jit(solution)/shard_map/ppermute | solution.py:176
  156.0 22.6 %collective-permute-start.15 = (bf16[5,384,128]{2,1,0:T(8,128)(2,1)S(1)}, bf16[5,384,128]{2,1,0:T(8,128)(2,1)S(1)}, u32[]{:S(2)}, u32[]{:S(2)}) collective-permute-start(bf16[5,384,128]{2,1,0:T(8,128)(2,1)S(1)} %get-tuple-element.20), channel_id=1, source_target_pairs={{0,16},{8,24},{16,0},{24,8},{1,17},{9,25},{17,1},{25,9},{2,18},{10... | collective-permute-start | bytes 1474568 | tf_op jit(solution)/shard_map/ppermute | solution.py:176
  157.5 22.9 %collective-permute-start.16 = (bf16[5,384,128]{2,1,0:T(8,128)(2,1)S(1)}, bf16[5,384,128]{2,1,0:T(8,128)(2,1)S(1)}, u32[]{:S(2)}, u32[]{:S(2)}) collective-permute-start(bf16[5,384,128]{2,1,0:T(8,128)(2,1)S(1)} %get-tuple-element.21), channel_id=1, source_target_pairs={{0,24},{8,16},{16,8},{24,0},{1,25},{9,17},{17,9},{25,1},{2,26},{10... | collective-permute-start | bytes 1474568 | tf_op jit(solution)/shard_map/ppermute | solution.py:176
  185.4 16.7 %copy-start.12 = (bf16[480,128]{1,0:T(8,128)(2,1)S(1)}, bf16[480,128]{1,0:T(8,128)(2,1)}, u32[]{:S(2)}) copy-start(bf16[480,128]{1,0:T(8,128)(2,1)} %copy-done.11) | copy-start | bytes 368644
  185.4 17.5 %collective-permute-start.20 = (bf16[4,640,640]{2,1,0:T(8,128)(2,1)}, bf16[4,640,640]{2,1,0:T(8,128)(2,1)}, u32[]{:S(2)}, u32[]{:S(2)}) collective-permute-start(bf16[4,640,640]{2,1,0:T(8,128)(2,1)} %after.16.refs_4_), channel_id=1, source_target_pairs={{0,1},{1,0},{2,3},{3,2},{4,5},{5,4},{6,7},{7,6},{8,9},{9,8},{10,11... | collective-permute-start | bytes 9830408 | tf_op jit(solution)/shard_map/ppermute | solution.py:176
  185.5 7.6 %collective-permute-start.17 = (bf16[480,128]{1,0:T(8,128)(2,1)S(1)}, bf16[480,128]{1,0:T(8,128)(2,1)S(1)}, u32[]{:S(2)}, u32[]{:S(2)}) collective-permute-start(bf16[480,128]{1,0:T(8,128)(2,1)S(1)} %get-tuple-element.24), channel_id=1, source_target_pairs={{0,6},{2,0},{4,2},{6,4},{1,7},{3,1},{5,3},{7,5},{8,14},{10,8},{12,... | collective-permute-start | bytes 368648 | tf_op jit(solution)/shard_map/ppermute | solution.py:171
  187.2 14.9 %collective-permute-start.18 = (bf16[480,128]{1,0:T(8,128)(2,1)S(1)}, bf16[480,128]{1,0:T(8,128)(2,1)S(1)}, u32[]{:S(2)}, u32[]{:S(2)}) collective-permute-start(bf16[480,128]{1,0:T(8,128)(2,1)S(1)} %get-tuple-element.25), channel_id=1, source_target_pairs={{0,4},{2,6},{4,0},{6,2},{1,5},{3,7},{5,1},{7,3},{8,12},{10,14},{12... | collective-permute-start | bytes 368648 | tf_op jit(solution)/shard_map/ppermute | solution.py:171
  190.6 11.6 %collective-permute-start.19 = (bf16[480,128]{1,0:T(8,128)(2,1)S(1)}, bf16[480,128]{1,0:T(8,128)(2,1)S(1)}, u32[]{:S(2)}, u32[]{:S(2)}) collective-permute-start(bf16[480,128]{1,0:T(8,128)(2,1)S(1)} %get-tuple-element.26), channel_id=1, source_target_pairs={{0,2},{2,4},{4,6},{6,0},{1,3},{3,5},{5,7},{7,1},{8,10},{10,12},{12... | collective-permute-start | bytes 368648 | tf_op jit(solution)/shard_map/ppermute | solution.py:171
  202.1 24.8 %copy-start.4 = (bf16[4,640,640]{2,1,0:T(8,128)(2,1)S(1)}, bf16[4,640,640]{2,1,0:T(8,128)(2,1)}, u32[]{:S(2)}) copy-start(bf16[4,640,640]{2,1,0:T(8,128)(2,1)} %after.16.refs_4_) | copy-start | bytes 9830404
  203.0 14.4 %collective-permute-start.21 = (bf16[4,480,128]{2,1,0:T(8,128)(2,1)}, bf16[4,480,128]{2,1,0:T(8,128)(2,1)}, u32[]{:S(2)}, u32[]{:S(2)}) collective-permute-start(bf16[4,480,128]{2,1,0:T(8,128)(2,1)} %after.17.refs_0_), channel_id=1, source_target_pairs={{0,8},{8,0},{16,24},{24,16},{1,9},{9,1},{17,25},{25,17},{2,10},{10... | collective-permute-start | bytes 1474568 | tf_op jit(solution)/shard_map/ppermute | solution.py:176
  203.5 23.4 %collective-permute-start.22 = (bf16[4,480,128]{2,1,0:T(8,128)(2,1)}, bf16[4,480,128]{2,1,0:T(8,128)(2,1)}, u32[]{:S(2)}, u32[]{:S(2)}) collective-permute-start(bf16[4,480,128]{2,1,0:T(8,128)(2,1)} %after.17.refs_0_), channel_id=1, source_target_pairs={{0,16},{8,24},{16,0},{24,8},{1,17},{9,25},{17,1},{25,9},{2,18},{10... | collective-permute-start | bytes 1474568 | tf_op jit(solution)/shard_map/ppermute | solution.py:176
  205.1 21.8 %collective-permute-start.23 = (bf16[4,480,128]{2,1,0:T(8,128)(2,1)}, bf16[4,480,128]{2,1,0:T(8,128)(2,1)}, u32[]{:S(2)}, u32[]{:S(2)}) collective-permute-start(bf16[4,480,128]{2,1,0:T(8,128)(2,1)} %after.17.refs_0_), channel_id=1, source_target_pairs={{0,24},{8,16},{16,8},{24,0},{1,25},{9,17},{17,9},{25,1},{2,26},{10... | collective-permute-start | bytes 1474568 | tf_op jit(solution)/shard_map/ppermute | solution.py:176
  236.9 8.9 %collective-permute-start.24 = (bf16[96,1280]{1,0:T(8,128)(2,1)S(1)}, bf16[96,1280]{1,0:T(8,128)(2,1)S(1)}, u32[]{:S(2)}, u32[]{:S(2)}) collective-permute-start(bf16[96,1280]{1,0:T(8,128)(2,1)S(1)} %get-tuple-element.28), channel_id=1, source_target_pairs={{0,8},{8,0},{16,24},{24,16},{1,9},{9,1},{17,25},{25,17},{2,10},{10... | collective-permute-start | bytes 737288 | tf_op jit(solution)/shard_map/ppermute | solution.py:176
  238.4 11.5 %collective-permute-start.25 = (bf16[96,1280]{1,0:T(8,128)(2,1)S(1)}, bf16[96,1280]{1,0:T(8,128)(2,1)S(1)}, u32[]{:S(2)}, u32[]{:S(2)}) collective-permute-start(bf16[96,1280]{1,0:T(8,128)(2,1)S(1)} %get-tuple-element.29), channel_id=1, source_target_pairs={{0,16},{8,24},{16,0},{24,8},{1,17},{9,25},{17,1},{25,9},{2,18},{10... | collective-permute-start | bytes 737288 | tf_op jit(solution)/shard_map/ppermute | solution.py:176
  239.0 10.9 %collective-permute-start.26 = (bf16[96,1280]{1,0:T(8,128)(2,1)S(1)}, bf16[96,1280]{1,0:T(8,128)(2,1)S(1)}, u32[]{:S(2)}, u32[]{:S(2)}) collective-permute-start(bf16[96,1280]{1,0:T(8,128)(2,1)S(1)} %get-tuple-element.30), channel_id=1, source_target_pairs={{0,24},{8,16},{16,8},{24,0},{1,25},{9,17},{17,9},{25,1},{2,26},{10... | collective-permute-start | bytes 737288 | tf_op jit(solution)/shard_map/ppermute | solution.py:176
  (18 other events, 56.9 us)
Sparse Core Ops, SparseCore 0:
  113.5 66.3 all-gather.2
where the time goes:
time: 260 us
  waiting for transfers between devices  132 us (51%)
  Pallas kernels  45.3 us (17%)
  starting transfers between devices  43.6 us (17%)
  local copies, waits for them, and re-layouts  19.6 us (8%)
  between operations  13.7 us (5%)
  other arithmetic  5.33 us (2%)
    ppermute x13, waiting for transfers between devices, across(): return lax.ppermute(value, axis, [(i, i ^ bits) for i in range(count)])  58.1 us
    ppermute x3, waiting for transfers between devices, hop(): lax.ppermute(upper, axis, [(i, i - 1) for i in range(1, count - s + 1)])  37.2 us
    pallas_call x2, Pallas kernels, project(): pl.pallas_call(body, out_shape=out_shape, grid_spec=pltpu.PrefetchScalarG...  22.4 us
    ppermute x1, waiting for transfers between devices, shards(): lax.ppermute(after(weight[FIRST_COLUMNS:], own), plane_axes, near_pairs)  14.3 us
    ppermute x13, starting transfers between devices, across(): return lax.ppermute(value, axis, [(i, i ^ bits) for i in range(count)])  11.1 us
    ppermute x3, waiting for transfers between devices, turn(): lax.ppermute(value, axis, [(i, (i + steps) % count) for i in range(count)])  10.8 us
    unnamed x45, local copies, waits for them, and re-layouts  9.67 us
    ppermute x1, waiting for transfers between devices, shards(): far = lax.ppermute(passed, plane_axes, far_pairs)  9.14 us
  transfers between devices with their start and end apart: 28, of which 15 were waited for; matrix products, arithmetic and copies ran while one was open for 5% of the time, Pallas kernels for 13%

commit v1 on v0

--- a/solution.py
+++ b/solution.py
@@ -645,6 +645,7 @@
     order = after(jnp.stack([here, here_near, here_other, here, core]), out_half)
     held = [("whole", (weight,)), ("columns", near), ("columns", other)]
     total = project(own, lower, upper, order, held, None, frames)
+    far = after(far, total)
     far = (far, across(far, "dp", 1))
     order = jnp.stack([here_far, here, core])
     *messages, last_query = project(

time: 260 us -> 250 us (0.962)
  waiting for transfers between devices: 132 us -> 125 us
  starting transfers between devices: 43.6 us -> 39.6 us
    ppermute x3, waiting for transfers between devices: 0.01 us -> 19.4 us  [hop(): lax.ppermute(lower, axis, [(i, i + 1) for i in range(s - 1, count - 1)])]
    ppermute x3, waiting for transfers between devices: 37.2 us -> 23 us  [hop(): lax.ppermute(upper, axis, [(i, i - 1) for i in range(1, count - s + 1)])]
    ppermute x1, waiting for transfers between devices: 9.14 us -> 0.01 us  [shards(): far = lax.ppermute(passed, plane_axes, far_pairs)]
    all_gather x1, waiting for transfers between devices: 0.01 us -> 2.7 us  [shards(): out_half = after(lax.all_gather(out_half, 'head'), outs[0])]
    unnamed x45 -> x47, local copies, waits for them, and re-layouts: 9.67 us -> 9.72 us
  transfers between devices with their start and end apart: 28 -> 28, of which waited for: 15 -> 15; matrix products, arithmetic and copies ran while one was open for 5% -> 6% of each run, Pallas kernels for 13% -> 14%
where the time goes in v1:
time: 250 us; the launch traced here: 249 us
  waiting for transfers between devices  125 us (50%)
  Pallas kernels  45.5 us (18%)
  starting transfers between devices  39.6 us (16%)
  local copies, waits for them, and re-layouts  19.7 us (8%)
  between operations  13.8 us (6%)
  other arithmetic  5.46 us (2%)
    ppermute x13, waiting for transfers between devices, across(): return lax.ppermute(value, axis, [(i, i ^ bits) for i in range(count)])  55.8 us
    ppermute x3, waiting for transfers between devices, hop(): lax.ppermute(upper, axis, [(i, i - 1) for i in range(1, count - s + 1)])  23 us
    pallas_call x2, Pallas kernels, project(): pl.pallas_call(body, out_shape=out_shape, grid_spec=pltpu.PrefetchScalarG...  22.7 us
    ppermute x3, waiting for transfers between devices, hop(): lax.ppermute(lower, axis, [(i, i + 1) for i in range(s - 1, count - 1)])  19.4 us
    ppermute x1, waiting for transfers between devices, shards(): lax.ppermute(after(weight[FIRST_COLUMNS:], own), plane_axes, near_pairs)  12.5 us
    ppermute x13, starting transfers between devices, across(): return lax.ppermute(value, axis, [(i, i ^ bits) for i in range(count)])  10.7 us
    unnamed x47, local copies, waits for them, and re-layouts  9.72 us
    ppermute x2, starting transfers between devices, shifted(): lax.ppermute(value, axis, [(source, source + steps) for source in range(l...  8.46 us
  transfers between devices with their start and end apart: 28, of which 15 were waited for; matrix products, arithmetic and copies ran while one was open for 6% of the time, Pallas kernels for 14%

profile of v1, /device:TPU:0, one launch (start us, length us, event | category | flops | bytes accessed | tf_op | source)
XLA Modules:
  0.0 248.6 jit_solution(10601352388873813374)
XLA Ops:
  6.5 4.8 %collective-permute-start = (bf16[2,4,48,256]{3,2,1,0:T(8,128)(2,1)}, bf16[2,4,48,256]{3,2,1,0:T(8,128)(2,1)S(1)}, u32[]{:S(2)}, u32[]{:S(2)}) collective-permute-start(bf16[2,4,48,256]{3,2,1,0:T(8,128)(2,1)} %param.10), channel_id=1, source_target_pairs={{0,8},{8,16},{16,24},{1,9},{9,17},{17,25},{2,10},{10,18},{18,26},{... | collective-permute-start | bytes 589832 | tf_op jit(solution)/shard_map/ppermute | solution.py:23
  13.1 2.7 %collective-permute-done.refs_1_ = bf16[2,4,48,256]{3,2,1,0:T(8,128)(2,1)S(1)} collective-permute-done((bf16[2,4,48,256]{3,2,1,0:T(8,128)(2,1)}, bf16[2,4,48,256]{3,2,1,0:T(8,128)(2,1)S(1)}, u32[]{:S(2)}, u32[]{:S(2)}) %collective-permute-start) | collective-permute-done | bytes 196640 | tf_op jit(solution)/shard_map/ppermute | solution.py:23
  17.0 3.6 %collective-permute-start.1 = (bf16[4,1,48,256]{3,2,1,0:T(8,128)(2,1)S(1)}, bf16[4,1,48,256]{3,2,1,0:T(8,128)(2,1)S(1)}, u32[]{:S(2)}, u32[]{:S(2)}) collective-permute-start(bf16[4,1,48,256]{3,2,1,0:T(8,128)(2,1)S(1)} %slice.16), channel_id=1, source_target_pairs={{0,2},{2,4},{4,6},{1,3},{3,5},{5,7},{8,10},{10,12},{12,14},{9,11},... | collective-permute-start | bytes 294920 | tf_op jit(solution)/shard_map/ppermute | solution.py:23
  20.6 3.3 %slice.19.refs_0_ = bf16[7,1280,128]{2,1,0:T(8,128)(2,1)} slice(bf16[15,1280,128]{2,1,0:T(8,128)(2,1)} %bitcast.41), slice={[8:15], [0:1280], [0:128]} | slice | bytes 4587520 | tf_op jit(solution)/shard_map/slice | solution.py:622
  25.6 2.4 collective-permute-start.4
  28.4 2.2 copy-done.8
  30.7 3.4 %pose_conv.1 = bf16[2,2,24,320]{3,2,1,0:T(8,128)(2,1)S(1)} custom-call(s32[6]{0:T(128)S(1)} %reshape.111.keep_ref, bf16[4,5,24,768]{3,2,1,0:T(8,128)(2,1)S(1)} %fusion.1.cols_ref, bf16[9,3,320,256]{3,2,1,0:T(8,128)(2,1)S(1)} %bitcast.37, f32[1,320]{1,0:T(1,128)S(1)} %reshape.106.bias_ref), custom_call_target="tpu_custom_call" | custom-call | flops 30720 | bytes 61440 | tf_op jit(solution)/shard_map/pose_conv/pallas_call | solution.py:274
  36.7 3.5 %collective-permute-start.2 = (bf16[96,5120]{1,0:T(8,128)(2,1)}, bf16[96,5120]{1,0:T(8,128)(2,1)S(1)}, u32[]{:S(2)}, u32[]{:S(2)}) collective-permute-start(bf16[96,5120]{1,0:T(8,128)(2,1)} %copy-done), channel_id=1, source_target_pairs={{0,2},{2,4},{4,6},{1,3},{3,5},{5,7},{8,10},{10,12},{12,14},{9,11},... | collective-permute-start | bytes 2949128 | tf_op jit(solution)/shard_map/ppermute | solution.py:181
  41.6 19.4 %collective-permute-done.2.refs_1_ = bf16[96,5120]{1,0:T(8,128)(2,1)S(1)} collective-permute-done((bf16[96,5120]{1,0:T(8,128)(2,1)}, bf16[96,5120]{1,0:T(8,128)(2,1)S(1)}, u32[]{:S(2)}, u32[]{:S(2)}) %collective-permute-start.2) | collective-permute-done | bytes 983072 | tf_op jit(solution)/shard_map/ppermute | solution.py:181
  62.7 2.5 %collective-permute-done.6.refs_2_.refs_4_ = bf16[96,5120]{1,0:T(8,128)(2,1)} collective-permute-done((bf16[96,5120]{1,0:T(8,128)(2,1)}, bf16[96,5120]{1,0:T(8,128)(2,1)}, u32[]{:S(2)}, u32[]{:S(2)}) %collective-permute-start.6) | collective-permute-done | bytes 983072 | tf_op jit(solution)/shard_map/ppermute | solution.py:182
  67.2 2.8 %take_block.1.refs_3_.refs_0_ = bf16[640,640]{1,0:T(8,128)(2,1)} custom-call(s32[2]{0:T(128)} %pad_add_fusion.2.at_ref, bf16[640,5120]{1,0:T(8,128)(2,1)} %bitcast.44), custom_call_target="tpu_custom_call" | custom-call | bytes 1638400 | tf_op jit(solution)/shard_map/take_block/pallas_call | solution.py:205
  70.0 12.5 %collective-permute-done.5.refs_0_ = bf16[7,1280,128]{2,1,0:T(8,128)(2,1)S(1)} collective-permute-done((bf16[7,1280,128]{2,1,0:T(8,128)(2,1)}, bf16[7,1280,128]{2,1,0:T(8,128)(2,1)S(1)}, u32[]{:S(2)}, u32[]{:S(2)}) %collective-permute-start.5) | collective-permute-done | bytes 2293792 | tf_op jit(solution)/shard_map/ppermute | solution.py:622
  86.7 1.7 pad_maximum_fusion.refs_1_
  88.4 1.7 collective-permute-start.7
  91.9 3.0 %collective-permute-start.10 = (bf16[15,640,128]{2,1,0:T(8,128)(2,1)}, bf16[15,640,128]{2,1,0:T(8,128)(2,1)}, u32[]{:S(2)}, u32[]{:S(2)}) collective-permute-start(bf16[15,640,128]{2,1,0:T(8,128)(2,1)} %pad_maximum_fusion.refs_1_), channel_id=1, source_target_pairs={{0,16},{1,9},{8,24},{9,1},{16,0},{17,25},{24,8},{25,17},{2,18},{3,... | collective-permute-start | bytes 7372808 | tf_op jit(solution)/shard_map/ppermute | solution.py:634
  94.9 20.4 %collective-permute-done.9.refs_2_.refs_6_ = bf16[96,5120]{1,0:T(8,128)(2,1)} collective-permute-done((bf16[96,5120]{1,0:T(8,128)(2,1)}, bf16[96,5120]{1,0:T(8,128)(2,1)}, u32[]{:S(2)}, u32[]{:S(2)}) %collective-permute-start.9) | collective-permute-done | bytes 983072 | tf_op jit(solution)/shard_map/ppermute | solution.py:182
  117.9 14.8 %project.2.refs_1_.refs_9_ = f32[384,1920]{1,0:T(8,128)} custom-call(s32[5]{0:T(128)S(1)} %copy-done.15, bf16[96,5120]{1,0:T(8,128)(2,1)S(1)} %copy-done.1, bf16[96,5120]{1,0:T(8,128)(2,1)S(1)} %copy-done.6, bf16[96,5120]{1,0:T(8,128)(2,1)} %after.13.refs_2_, bf16[96,5120]{1,0:T(8,128)(2,1)} %collective-permute-done.7.refs_1_.refs_3_, ...), custom_call_target="tpu_custom_call" | custom-call | bytes 98304 | tf_op jit(solution)/shard_map/project/pallas_call | solution.py:441
  132.9 4.9 %collective-permute-done.13.refs_8_ = bf16[15,640,128]{2,1,0:T(8,128)(2,1)} collective-permute-done((bf16[15,640,128]{2,1,0:T(8,128)(2,1)}, bf16[15,640,128]{2,1,0:T(8,128)(2,1)}, u32[]{:S(2)}, u32[]{:S(2)}) %collective-permute-start.13) | collective-permute-done | bytes 2457632 | tf_op jit(solution)/shard_map/ppermute | solution.py:176
  137.8 8.0 %project.3 = (bf16[5,384,128]{2,1,0:T(8,128)(2,1)S(1)}, bf16[5,384,128]{2,1,0:T(8,128)(2,1)}, bf16[5,384,128]{2,1,0:T(8,128)(2,1)S(1)}, bf16[5,384,128]{2,1,0:T(8,128)(2,1)S(1)}, bf16[384,128]{1,0:T(8,128)(2,1)S(1)}) custom-call(s32[3]{0:T(128)S(1)} %add_add_fusion.1.order_ref, bf16[96,5120]{1,0:T(8,128)(2,1)S(1)} %copy-done.1, ...), custom_call_target="tpu_custom_call" | custom-call | bytes 98304 | tf_op jit(solution)/shard_map/project/pallas_call | solution.py:441
  149.8 10.3 %collective-permute-done.14.refs_1_ = bf16[5,384,128]{2,1,0:T(8,128)(2,1)S(1)} collective-permute-done((bf16[5,384,128]{2,1,0:T(8,128)(2,1)}, bf16[5,384,128]{2,1,0:T(8,128)(2,1)S(1)}, u32[]{:S(2)}, u32[]{:S(2)}) %collective-permute-start.14) | collective-permute-done | bytes 491552 | tf_op jit(solution)/shard_map/ppermute | solution.py:176
  160.1 10.9 %collective-permute-done.16.refs_3_ = bf16[5,384,128]{2,1,0:T(8,128)(2,1)S(1)} collective-permute-done((bf16[5,384,128]{2,1,0:T(8,128)(2,1)S(1)}, bf16[5,384,128]{2,1,0:T(8,128)(2,1)S(1)}, u32[]{:S(2)}, u32[]{:S(2)}) %collective-permute-start.16) | collective-permute-done | bytes 491552 | tf_op jit(solution)/shard_map/ppermute | solution.py:176
  171.0 4.3 %attend.1 = (bf16[480,128]{1,0:T(8,128)(2,1)S(1)}, bf16[480,128]{1,0:T(8,128)(2,1)S(1)}, bf16[480,128]{1,0:T(8,128)(2,1)S(1)}, bf16[480,128]{1,0:T(8,128)(2,1)S(1)}) custom-call(s32[25]{0:T(128)S(1)} %pad_add_fusion.1.table_ref, bf16[5,384,128]{2,1,0:T(8,128)(2,1)S(1)} %get-tuple-element.18.refs_0_, ...), custom_call_target="tpu_custom_call" | custom-call | bytes 98304 | tf_op jit(solution)/shard_map/attend/pallas_call | solution.py:498
  176.0 2.7 %all-gather.3.cloned.1.call-done = bf16[2560,640]{1,0:T(8,128)(2,1)} async-done(((bf16[640,640]{1,0:T(8,128)(2,1)}), bf16[2560,640]{1,0:T(8,128)(2,1)}) %all-gather.3.cloned.1.call-update) | async-done | bytes 3276816 | tf_op jit(solution)/shard_map/all_gather | solution.py:663
  180.0 2.7 %collective-permute-start.17 = (bf16[480,128]{1,0:T(8,128)(2,1)S(1)}, bf16[480,128]{1,0:T(8,128)(2,1)S(1)}, u32[]{:S(2)}, u32[]{:S(2)}) collective-permute-start(bf16[480,128]{1,0:T(8,128)(2,1)S(1)} %get-tuple-element.24), channel_id=1, source_target_pairs={{0,6},{2,0},{4,2},{6,4},{1,7},{3,1},{5,3},{7,5},{8,14},{10,8},{12,... | collective-permute-start | bytes 368648 | tf_op jit(solution)/shard_map/ppermute | solution.py:171
  182.7 4.1 %collective-permute-done.19 = bf16[480,128]{1,0:T(8,128)(2,1)S(1)} collective-permute-done((bf16[480,128]{1,0:T(8,128)(2,1)S(1)}, bf16[480,128]{1,0:T(8,128)(2,1)S(1)}, u32[]{:S(2)}, u32[]{:S(2)}) %collective-permute-start.19) | collective-permute-done | bytes 122912 | tf_op jit(solution)/shard_map/ppermute | solution.py:171
  186.8 4.3 %collective-permute-done.18 = bf16[480,128]{1,0:T(8,128)(2,1)S(1)} collective-permute-done((bf16[480,128]{1,0:T(8,128)(2,1)S(1)}, bf16[480,128]{1,0:T(8,128)(2,1)S(1)}, u32[]{:S(2)}, u32[]{:S(2)}) %collective-permute-start.18) | collective-permute-done | bytes 122912 | tf_op jit(solution)/shard_map/ppermute | solution.py:171
  195.6 10.9 %collective-permute-done.21.refs_1_ = bf16[4,480,128]{2,1,0:T(8,128)(2,1)} collective-permute-done((bf16[4,480,128]{2,1,0:T(8,128)(2,1)}, bf16[4,480,128]{2,1,0:T(8,128)(2,1)}, u32[]{:S(2)}, u32[]{:S(2)}) %collective-permute-start.21) | collective-permute-done | bytes 491552 | tf_op jit(solution)/shard_map/ppermute | solution.py:176
  206.5 9.9 %collective-permute-done.22.refs_2_ = bf16[4,480,128]{2,1,0:T(8,128)(2,1)} collective-permute-done((bf16[4,480,128]{2,1,0:T(8,128)(2,1)}, bf16[4,480,128]{2,1,0:T(8,128)(2,1)}, u32[]{:S(2)}, u32[]{:S(2)}) %collective-permute-start.22) | collective-permute-done | bytes 491552 | tf_op jit(solution)/shard_map/ppermute | solution.py:176
  217.4 8.3 %out_project.1 = (bf16[96,1280]{1,0:T(8,128)(2,1)S(1)}, bf16[96,1280]{1,0:T(8,128)(2,1)S(1)}, bf16[96,1280]{1,0:T(8,128)(2,1)S(1)}, bf16[96,1280]{1,0:T(8,128)(2,1)S(1)}) custom-call(s32[3]{0:T(128)S(1)} %add_add_fusion.at_ref, bf16[4,480,128]{2,1,0:T(8,128)(2,1)S(1)} %copy-done.9, bf16[4,480,128]{2,1,0:T(8,128)(2,1)} %collective-permute-done.21.refs_1_, ...), custom_call_target="tpu_custom_call" | custom-call | bytes 983040 | tf_op jit(solution)/shard_map/out_project/pallas_call | solution.py:558
  229.9 5.0 %collective-permute-done.24.refs_1_ = bf16[96,1280]{1,0:T(8,128)(2,1)S(1)} collective-permute-done((bf16[96,1280]{1,0:T(8,128)(2,1)S(1)}, bf16[96,1280]{1,0:T(8,128)(2,1)S(1)}, u32[]{:S(2)}, u32[]{:S(2)}) %collective-permute-start.24) | collective-permute-done | bytes 245792 | tf_op jit(solution)/shard_map/ppermute | solution.py:176
  234.9 3.8 %collective-permute-done.25.refs_2_ = bf16[96,1280]{1,0:T(8,128)(2,1)S(1)} collective-permute-done((bf16[96,1280]{1,0:T(8,128)(2,1)S(1)}, bf16[96,1280]{1,0:T(8,128)(2,1)S(1)}, u32[]{:S(2)}, u32[]{:S(2)}) %collective-permute-start.25) | collective-permute-done | bytes 245792 | tf_op jit(solution)/shard_map/ppermute | solution.py:176
  239.5 2.3 place_columns.1
  (121 shorter events, 37.5 us)
Async XLA Ops:
  6.5 172.2 %all-gather.3.cloned.1.call-start = ((), (), s32[]{:S(2)}) async-start(), calls=%async_computation | async-start | bytes 4096000 | tf_op jit(solution)/shard_map/all_gather | solution.py:663
  6.5 9.3 %collective-permute-start = (bf16[2,4,48,256]{3,2,1,0:T(8,128)(2,1)}, bf16[2,4,48,256]{3,2,1,0:T(8,128)(2,1)S(1)}, u32[]{:S(2)}, u32[]{:S(2)}) collective-permute-start(bf16[2,4,48,256]{3,2,1,0:T(8,128)(2,1)} %param.10), channel_id=1, source_target_pairs={{0,8},{8,16},{16,24},{1,9},{9,17},{17,25},{2,10},{10,18},{18,26},{... | collective-permute-start | bytes 589832 | tf_op jit(solution)/shard_map/ppermute | solution.py:23
  17.0 11.1 %collective-permute-start.1 = (bf16[4,1,48,256]{3,2,1,0:T(8,128)(2,1)S(1)}, bf16[4,1,48,256]{3,2,1,0:T(8,128)(2,1)S(1)}, u32[]{:S(2)}, u32[]{:S(2)}) collective-permute-start(bf16[4,1,48,256]{3,2,1,0:T(8,128)(2,1)S(1)} %slice.16), channel_id=1, source_target_pairs={{0,2},{2,4},{4,6},{1,3},{3,5},{5,7},{8,10},{10,12},{12,14},{9,11},... | collective-permute-start | bytes 294920 | tf_op jit(solution)/shard_map/ppermute | solution.py:23
  25.6 59.7 %collective-permute-start.4 = (bf16[8,1280,128]{2,1,0:T(8,128)(2,1)}, bf16[8,1280,128]{2,1,0:T(8,128)(2,1)}, u32[]{:S(2)}, u32[]{:S(2)}) collective-permute-start(bf16[8,1280,128]{2,1,0:T(8,128)(2,1)} %after.10), channel_id=1, source_target_pairs={{0,8},{1,17},{8,0},{9,25},{16,24},{17,1},{24,16},{25,9},{2,10},{3,... | collective-permute-start | bytes 7864328 | tf_op jit(solution)/shard_map/ppermute | solution.py:617
  36.7 45.8 %collective-permute-start.5 = (bf16[7,1280,128]{2,1,0:T(8,128)(2,1)}, bf16[7,1280,128]{2,1,0:T(8,128)(2,1)S(1)}, u32[]{:S(2)}, u32[]{:S(2)}) collective-permute-start(bf16[7,1280,128]{2,1,0:T(8,128)(2,1)} %after.11), channel_id=1, source_target_pairs={{0,8},{1,17},{8,0},{9,25},{16,24},{17,1},{24,16},{25,9},{2,10},{3,... | collective-permute-start | bytes 6881288 | tf_op jit(solution)/shard_map/ppermute | solution.py:622
  36.7 24.3 %collective-permute-start.2 = (bf16[96,5120]{1,0:T(8,128)(2,1)}, bf16[96,5120]{1,0:T(8,128)(2,1)S(1)}, u32[]{:S(2)}, u32[]{:S(2)}) collective-permute-start(bf16[96,5120]{1,0:T(8,128)(2,1)} %copy-done), channel_id=1, source_target_pairs={{0,2},{2,4},{4,6},{1,3},{3,5},{5,7},{8,10},{10,12},{12,14},{9,11},... | collective-permute-start | bytes 2949128 | tf_op jit(solution)/shard_map/ppermute | solution.py:181
  40.3 24.9 %collective-permute-start.6 = (bf16[96,5120]{1,0:T(8,128)(2,1)}, bf16[96,5120]{1,0:T(8,128)(2,1)}, u32[]{:S(2)}, u32[]{:S(2)}) collective-permute-start(bf16[96,5120]{1,0:T(8,128)(2,1)} %copy-done), channel_id=1, source_target_pairs={{2,0},{4,2},{6,4},{3,1},{5,3},{7,5},{10,8},{12,10},{14,12},{11,9},... | collective-permute-start | bytes 2949128 | tf_op jit(solution)/shard_map/ppermute | solution.py:182
  61.0 27.4 %collective-permute-start.3 = (bf16[96,5120]{1,0:T(8,128)(2,1)S(1)}, bf16[96,5120]{1,0:T(8,128)(2,1)}, u32[]{:S(2)}, u32[]{:S(2)}) collective-permute-start(bf16[96,5120]{1,0:T(8,128)(2,1)S(1)} %collective-permute-done.2.refs_1_), channel_id=1, source_target_pairs={{2,4},{4,6},{3,5},{5,7},{10,12},{12,14},{11,13},{13,15},{18,20},{2... | collective-permute-start | bytes 2949128 | tf_op jit(solution)/shard_map/ppermute | solution.py:181
  65.2 25.0 %collective-permute-start.8 = (bf16[96,5120]{1,0:T(8,128)(2,1)}, bf16[96,5120]{1,0:T(8,128)(2,1)}, u32[]{:S(2)}, u32[]{:S(2)}) collective-permute-start(bf16[96,5120]{1,0:T(8,128)(2,1)} %collective-permute-done.6.refs_2_.refs_4_), channel_id=1, source_target_pairs={{2,0},{4,2},{3,1},{5,3},{10,8},{12,10},{11,9},{13,11},{18,16},{20,... | collective-permute-start | bytes 2949128 | tf_op jit(solution)/shard_map/ppermute | solution.py:182
  88.4 6.5 %collective-permute-start.7 = (bf16[96,5120]{1,0:T(8,128)(2,1)}, bf16[96,5120]{1,0:T(8,128)(2,1)}, u32[]{:S(2)}, u32[]{:S(2)}) collective-permute-start(bf16[96,5120]{1,0:T(8,128)(2,1)} %after.13.refs_2_), channel_id=1, source_target_pairs={{4,6},{5,7},{12,14},{13,15},{20,22},{21,23},{28,30},{29,31}} | collective-permute-start | bytes 2949128 | tf_op jit(solution)/shard_map/ppermute | solution.py:181
  90.2 25.8 %copy-start.1 = (bf16[96,5120]{1,0:T(8,128)(2,1)S(1)}, bf16[96,5120]{1,0:T(8,128)(2,1)}, u32[]{:S(2)}) copy-start(bf16[96,5120]{1,0:T(8,128)(2,1)} %copy-done) | copy-start | bytes 2949124
  90.2 25.1 %collective-permute-start.9 = (bf16[96,5120]{1,0:T(8,128)(2,1)}, bf16[96,5120]{1,0:T(8,128)(2,1)}, u32[]{:S(2)}, u32[]{:S(2)}) collective-permute-start(bf16[96,5120]{1,0:T(8,128)(2,1)} %after.14.refs_5_), channel_id=1, source_target_pairs={{2,0},{3,1},{10,8},{11,9},{18,16},{19,17},{26,24},{27,25}} | collective-permute-start | bytes 2949128 | tf_op jit(solution)/shard_map/ppermute | solution.py:182
  91.8 24.2 %collective-permute-start.11 = (bf16[8,1280,128]{2,1,0:T(8,128)(2,1)}, bf16[8,1280,128]{2,1,0:T(8,128)(2,1)}, u32[]{:S(2)}, u32[]{:S(2)}) collective-permute-start(bf16[8,1280,128]{2,1,0:T(8,128)(2,1)} %collective-permute-done.4.refs_8_), channel_id=1, source_target_pairs={{0,1},{1,0},{2,3},{3,2},{4,5},{5,4},{6,7},{7,6},{8,9},{9,8},{10,11... | collective-permute-start | bytes 7864328 | tf_op jit(solution)/shard_map/ppermute | solution.py:176
  91.9 40.8 %collective-permute-start.10 = (bf16[15,640,128]{2,1,0:T(8,128)(2,1)}, bf16[15,640,128]{2,1,0:T(8,128)(2,1)}, u32[]{:S(2)}, u32[]{:S(2)}) collective-permute-start(bf16[15,640,128]{2,1,0:T(8,128)(2,1)} %pad_maximum_fusion.refs_1_), channel_id=1, source_target_pairs={{0,16},{1,9},{8,24},{9,1},{16,0},{17,25},{24,8},{25,17},{2,18},{3,... | collective-permute-start | bytes 7372808 | tf_op jit(solution)/shard_map/ppermute | solution.py:634
  94.9 21.1 %collective-permute-start.12 = (bf16[7,1280,128]{2,1,0:T(8,128)(2,1)S(1)}, bf16[7,1280,128]{2,1,0:T(8,128)(2,1)}, u32[]{:S(2)}, u32[]{:S(2)}) collective-permute-start(bf16[7,1280,128]{2,1,0:T(8,128)(2,1)S(1)} %copy-done.3), channel_id=1, source_target_pairs={{0,1},{1,0},{2,3},{3,2},{4,5},{5,4},{6,7},{7,6},{8,9},{9,8},{10,11... | collective-permute-start | bytes 6881288 | tf_op jit(solution)/shard_map/ppermute | solution.py:176
  132.7 5.1 %collective-permute-start.13 = (bf16[15,640,128]{2,1,0:T(8,128)(2,1)}, bf16[15,640,128]{2,1,0:T(8,128)(2,1)}, u32[]{:S(2)}, u32[]{:S(2)}) collective-permute-start(bf16[15,640,128]{2,1,0:T(8,128)(2,1)} %after.17.refs_7_), channel_id=1, source_target_pairs={{0,1},{1,0},{2,3},{3,2},{4,5},{5,4},{6,7},{7,6},{8,9},{9,8},{10,11... | collective-permute-start | bytes 7372808 | tf_op jit(solution)/shard_map/ppermute | solution.py:176
  132.9 16.4 %copy-start.22 = (s32[8]{0:T(128)S(1)}, s32[8]{0:T(128)}, u32[]{:S(2)}) copy-start(s32[8]{0:T(128)} %param.17) | copy-start | bytes 100
  145.8 14.3 %collective-permute-start.14 = (bf16[5,384,128]{2,1,0:T(8,128)(2,1)}, bf16[5,384,128]{2,1,0:T(8,128)(2,1)S(1)}, u32[]{:S(2)}, u32[]{:S(2)}) collective-permute-start(bf16[5,384,128]{2,1,0:T(8,128)(2,1)} %get-tuple-element.19), channel_id=1, source_target_pairs={{0,8},{8,0},{16,24},{24,16},{1,9},{9,1},{17,25},{25,17},{2,10},{10... | collective-permute-start | bytes 1474568 | tf_op jit(solution)/shard_map/ppermute | solution.py:176
  146.5 13.7 %collective-permute-start.15 = (bf16[5,384,128]{2,1,0:T(8,128)(2,1)S(1)}, bf16[5,384,128]{2,1,0:T(8,128)(2,1)S(1)}, u32[]{:S(2)}, u32[]{:S(2)}) collective-permute-start(bf16[5,384,128]{2,1,0:T(8,128)(2,1)S(1)} %get-tuple-element.20), channel_id=1, source_target_pairs={{0,16},{8,24},{16,0},{24,8},{1,17},{9,25},{17,1},{25,9},{2,18},{10... | collective-permute-start | bytes 1474568 | tf_op jit(solution)/shard_map/ppermute | solution.py:176
  148.0 23.0 %collective-permute-start.16 = (bf16[5,384,128]{2,1,0:T(8,128)(2,1)S(1)}, bf16[5,384,128]{2,1,0:T(8,128)(2,1)S(1)}, u32[]{:S(2)}, u32[]{:S(2)}) collective-permute-start(bf16[5,384,128]{2,1,0:T(8,128)(2,1)S(1)} %get-tuple-element.21), channel_id=1, source_target_pairs={{0,24},{8,16},{16,8},{24,0},{1,25},{9,17},{17,9},{25,1},{2,26},{10... | collective-permute-start | bytes 1474568 | tf_op jit(solution)/shard_map/ppermute | solution.py:176
  178.7 12.4 %copy-start.13 = (bf16[480,128]{1,0:T(8,128)(2,1)S(1)}, bf16[480,128]{1,0:T(8,128)(2,1)}, u32[]{:S(2)}) copy-start(bf16[480,128]{1,0:T(8,128)(2,1)} %copy-done.12) | copy-start | bytes 368644
  178.7 13.3 %collective-permute-start.20 = (bf16[4,640,640]{2,1,0:T(8,128)(2,1)}, bf16[4,640,640]{2,1,0:T(8,128)(2,1)}, u32[]{:S(2)}, u32[]{:S(2)}) collective-permute-start(bf16[4,640,640]{2,1,0:T(8,128)(2,1)} %after.18.refs_4_), channel_id=1, source_target_pairs={{0,1},{1,0},{2,3},{3,2},{4,5},{5,4},{6,7},{7,6},{8,9},{9,8},{10,11... | collective-permute-start | bytes 9830408 | tf_op jit(solution)/shard_map/ppermute | solution.py:176
  178.7 8.1 %collective-permute-start.19 = (bf16[480,128]{1,0:T(8,128)(2,1)S(1)}, bf16[480,128]{1,0:T(8,128)(2,1)S(1)}, u32[]{:S(2)}, u32[]{:S(2)}) collective-permute-start(bf16[480,128]{1,0:T(8,128)(2,1)S(1)} %get-tuple-element.26), channel_id=1, source_target_pairs={{0,2},{2,4},{4,6},{6,0},{1,3},{3,5},{5,7},{7,1},{8,10},{10,12},{12... | collective-permute-start | bytes 368648 | tf_op jit(solution)/shard_map/ppermute | solution.py:171
  178.7 12.4 %collective-permute-start.18 = (bf16[480,128]{1,0:T(8,128)(2,1)S(1)}, bf16[480,128]{1,0:T(8,128)(2,1)S(1)}, u32[]{:S(2)}, u32[]{:S(2)}) collective-permute-start(bf16[480,128]{1,0:T(8,128)(2,1)S(1)} %get-tuple-element.25), channel_id=1, source_target_pairs={{0,4},{2,6},{4,0},{6,2},{1,5},{3,7},{5,1},{7,3},{8,12},{10,14},{12... | collective-permute-start | bytes 368648 | tf_op jit(solution)/shard_map/ppermute | solution.py:171
  180.0 11.1 %collective-permute-start.17 = (bf16[480,128]{1,0:T(8,128)(2,1)S(1)}, bf16[480,128]{1,0:T(8,128)(2,1)S(1)}, u32[]{:S(2)}, u32[]{:S(2)}) collective-permute-start(bf16[480,128]{1,0:T(8,128)(2,1)S(1)} %get-tuple-element.24), channel_id=1, source_target_pairs={{0,6},{2,0},{4,2},{6,4},{1,7},{3,1},{5,3},{7,5},{8,14},{10,8},{12,... | collective-permute-start | bytes 368648 | tf_op jit(solution)/shard_map/ppermute | solution.py:171
  191.1 25.2 %copy-start.4 = (bf16[4,640,640]{2,1,0:T(8,128)(2,1)S(1)}, bf16[4,640,640]{2,1,0:T(8,128)(2,1)}, u32[]{:S(2)}) copy-start(bf16[4,640,640]{2,1,0:T(8,128)(2,1)} %after.18.refs_4_) | copy-start | bytes 9830404
  192.0 14.5 %collective-permute-start.21 = (bf16[4,480,128]{2,1,0:T(8,128)(2,1)}, bf16[4,480,128]{2,1,0:T(8,128)(2,1)}, u32[]{:S(2)}, u32[]{:S(2)}) collective-permute-start(bf16[4,480,128]{2,1,0:T(8,128)(2,1)} %after.19.refs_0_), channel_id=1, source_target_pairs={{0,8},{8,0},{16,24},{24,16},{1,9},{9,1},{17,25},{25,17},{2,10},{10... | collective-permute-start | bytes 1474568 | tf_op jit(solution)/shard_map/ppermute | solution.py:176
  193.5 22.9 %collective-permute-start.22 = (bf16[4,480,128]{2,1,0:T(8,128)(2,1)}, bf16[4,480,128]{2,1,0:T(8,128)(2,1)}, u32[]{:S(2)}, u32[]{:S(2)}) collective-permute-start(bf16[4,480,128]{2,1,0:T(8,128)(2,1)} %after.19.refs_0_), channel_id=1, source_target_pairs={{0,16},{8,24},{16,0},{24,8},{1,17},{9,25},{17,1},{25,9},{2,18},{10... | collective-permute-start | bytes 1474568 | tf_op jit(solution)/shard_map/ppermute | solution.py:176
  194.9 21.4 %collective-permute-start.23 = (bf16[4,480,128]{2,1,0:T(8,128)(2,1)}, bf16[4,480,128]{2,1,0:T(8,128)(2,1)}, u32[]{:S(2)}, u32[]{:S(2)}) collective-permute-start(bf16[4,480,128]{2,1,0:T(8,128)(2,1)} %after.19.refs_0_), channel_id=1, source_target_pairs={{0,24},{8,16},{16,8},{24,0},{1,25},{9,17},{17,9},{25,1},{2,26},{10... | collective-permute-start | bytes 1474568 | tf_op jit(solution)/shard_map/ppermute | solution.py:176
  226.4 8.5 %collective-permute-start.24 = (bf16[96,1280]{1,0:T(8,128)(2,1)S(1)}, bf16[96,1280]{1,0:T(8,128)(2,1)S(1)}, u32[]{:S(2)}, u32[]{:S(2)}) collective-permute-start(bf16[96,1280]{1,0:T(8,128)(2,1)S(1)} %get-tuple-element.28), channel_id=1, source_target_pairs={{0,8},{8,0},{16,24},{24,16},{1,9},{9,1},{17,25},{25,17},{2,10},{10... | collective-permute-start | bytes 737288 | tf_op jit(solution)/shard_map/ppermute | solution.py:176
  227.6 11.1 %collective-permute-start.25 = (bf16[96,1280]{1,0:T(8,128)(2,1)S(1)}, bf16[96,1280]{1,0:T(8,128)(2,1)S(1)}, u32[]{:S(2)}, u32[]{:S(2)}) collective-permute-start(bf16[96,1280]{1,0:T(8,128)(2,1)S(1)} %get-tuple-element.29), channel_id=1, source_target_pairs={{0,16},{8,24},{16,0},{24,8},{1,17},{9,25},{17,1},{25,9},{2,18},{10... | collective-permute-start | bytes 737288 | tf_op jit(solution)/shard_map/ppermute | solution.py:176
  228.4 10.3 %collective-permute-start.26 = (bf16[96,1280]{1,0:T(8,128)(2,1)S(1)}, bf16[96,1280]{1,0:T(8,128)(2,1)S(1)}, u32[]{:S(2)}, u32[]{:S(2)}) collective-permute-start(bf16[96,1280]{1,0:T(8,128)(2,1)S(1)} %get-tuple-element.30), channel_id=1, source_target_pairs={{0,24},{8,16},{16,8},{24,0},{1,25},{9,17},{17,9},{25,1},{2,26},{10... | collective-permute-start | bytes 737288 | tf_op jit(solution)/shard_map/ppermute | solution.py:176
  (19 other events, 59.3 us)
Sparse Core Ops, SparseCore 0:
  115.5 63.1 all-gather.2
